TPU v7x, 128 devices: a whole 4x4x4 slice. The times are simulated.
128 devices in a mesh: cell: 32 (over y, z, core), wall: 4 (over x).
Axes of the slice: x: 4, y: 4, z: 4, core: 2. Of those that a mesh axis runs over, the one named last changes fastest.
Arguments:
- cell_points: float32 [1024, 3, 544], P('cell'), may hold values from -4 to 4
- cell_density: float32 [1024, 3, 544], P('cell'), may hold values from -6 to 6
- cell_weights: float32 [1024, 544], P('cell'), may hold values from 0.1 to 1
- near_device: int32 [1024, 8], P('cell'), may hold values from 0 to 31, all different within a row; in each aligned block of 32 rows (0 to 31, 32 to 63, ...) at most 16 rows name the same one
- near_slot: int32 [1024, 8], P('cell'), may hold values from 0 to 31
- near_wall: int32 [1024, 8], P('cell'), may hold values from 0 to 255
- wall_points: float32 [8192, 3, 256], P(('cell', 'wall')), may hold values from -4 to 4
- wall_density: float32 [8192, 3, 256], P(('cell', 'wall')), may hold values from -6 to 6
- wall_weights: float32 [8192, 256], P(('cell', 'wall')), may hold values from 0.1 to 1
Outputs:
- cell_velocity: float32 [1024, 3, 544], P('cell', None, 'wall')
- wall_velocity: float32 [8192, 3, 256], P(('cell', 'wall'))
Inputs may be any that keep to these rules, and one draw needn't show every extreme that they name: `near_device`: the 8 entries of a row are distinct. Among the rows of one index of cell (32 rows) no value is named more than 16 times, a bound that some block reaches.
All inputs are finite; a program needn't handle non-finite values.
Results may differ from a plain program's by a relative error of at most 0.00005.
Values sent between devices are 32-bit elements; how exact they have to be, the bound alone decides.
A program may use at most 128 MiB of HBM per device.

v0:
```python
import jax
import jax.numpy as jnp
from jax import lax
from jax.experimental import pallas as pl
from jax.experimental.pallas import tpu as pltpu
from jax.sharding import PartitionSpec as P

f32 = jnp.float32
bf16 = jnp.bfloat16
two_stokes_factor = 2.0 * 0.039788735772973836
levels = ((1, 1), (1, 2), (1, 3), (2, 1), (2, 2), (3, 1))
depth = 64
lanes = 128


def split3(x):
    first = x.astype(bf16).astype(f32)
    rest = x - first
    second = rest.astype(bf16).astype(f32)
    return first, second, rest - second


def source_features(raw):
    y = [raw[i : i + 1, :] for i in range(3)]
    g = [raw[i : i + 1, :] for i in range(3, 6)]
    square = y[0] * y[0] + y[1] * y[1] + y[2] * y[2] + 1.0
    dot = g[0] * y[0] + g[1] * y[1] + g[2] * y[2]
    rows = jnp.concatenate(
        [-2.0 * y[0], -2.0 * y[1], -2.0 * y[2], square, g[0], g[1], g[2], -dot], axis=0
    )
    parts = split3(rows)
    one = jnp.ones_like(rows)
    stack = [parts[p - 1] for p, _ in levels] + [one, jnp.zeros_like(rows)]
    return jnp.concatenate(stack, axis=0).astype(bf16)


def prepare_own(j, point_ref, density_ref, weight_ref, feature_ref, own_ref, a_ref, kinds):
    points = point_ref.shape[2]
    x = 2.0 * point_ref[j]
    center = jnp.sum(x, axis=1, keepdims=True) * (1.0 / points)
    x = x - center
    load = density_ref[j] * weight_ref[pl.ds(j, 1), :]
    own_ref[0:3, :points] = x
    own_ref[3:6, :points] = load
    xs = split3(x)
    squares = split3(jnp.sum(x * x, axis=0, keepdims=True))
    for i, (_, q) in enumerate(levels):
        feature_ref[8 * i : 8 * i + 3, :points] = xs[q - 1]
        feature_ref[depth + 8 * i + 4 : depth + 8 * i + 7, :points] = xs[q - 1]
    for i in range(3):
        feature_ref[48 + i : 49 + i, :points] = squares[i]
    if kinds == 3:
        ls = split3(-0.5 * load)
        dots = split3(-jnp.sum(x * load, axis=0, keepdims=True))
        for i, (_, q) in enumerate(levels):
            feature_ref[2 * depth + 8 * i : 2 * depth + 8 * i + 3, :points] = ls[q - 1]
        for i in range(3):
            feature_ref[2 * depth + 48 + i : 2 * depth + 49 + i, :points] = dots[i]
    for kind in range(kinds):
        turned = feature_ref[kind * depth : kind * depth + depth, :].T
        a_ref[kind * points : kind * points + points, :] = turned[:points].astype(bf16)
    return jnp.concatenate([jnp.broadcast_to(center, (3, lanes)), jnp.zeros((5, lanes), f32)], axis=0)


def start_features(feature_ref):
    feature_ref[...] = jnp.zeros_like(feature_ref)
    one = jnp.ones((1, feature_ref.shape[1]), f32)
    for i, (_, q) in enumerate(levels):
        if q == 1:
            feature_ref[8 * i + 3 : 8 * i + 4, :] = one
            feature_ref[depth + 8 * i + 7 : depth + 8 * i + 8, :] = one


def products(a_ref, w_ref, s_ref):
    n = w_ref.shape[1]
    for c in range(0, n, 256):
        e = min(n, c + 256)
        s_ref[:, c:e] = jnp.dot(a_ref[...], w_ref[:, c:e], preferred_element_type=f32)


def source_rows(r_ref, cols):
    return [jnp.broadcast_to(r_ref[i : i + 1, cols], (8, lanes)) for i in range(6)]


def added(total, term):
    return term if total is None else total + term


def near_kernel(
    ids_ref,
    gathered_ref,
    point_ref,
    density_ref,
    weight_ref,
    wall_ref,
    out_ref,
    s0,
    s1,
    r0,
    r1,
    w0,
    w1,
    o0,
    o1,
    a0,
    a1,
    feature_ref,
    sums,
):
    cells = out_ref.shape[0]
    points = out_ref.shape[2]
    tiles = r0.shape[1] // lanes

    def prepare(j, center, r_ref, w_ref):
        lane = lax.broadcasted_iota(jnp.int32, (8, lanes), 1)
        tail = jnp.zeros((8, lanes), f32)
        parts = []
        for k in range(8):
            block = gathered_ref[ids_ref[j, k]]
            parts.append(block - center)
            last = jnp.broadcast_to(block[6:7, :], (8, lanes))
            last = pltpu.roll(last, 8 * k, 1, stride=8, stride_axis=0)
            tail = jnp.where((lane >= 8 * k) & (lane < 8 * k + 8), last, tail)
        parts.append(jnp.where(lane < 64, tail - center, 0.0))
        raw = jnp.concatenate(parts, axis=1)
        r_ref[...] = raw
        w_ref[...] = source_features(raw)

    def evaluate(j, s_ref, r_ref, own_ref):
        blocks = 4
        for start in range(0, points, 8 * blocks):
            acc = [[None] * blocks for _ in range(4)]
            for c in range(tiles):
                cols = slice(c * lanes, c * lanes + lanes)
                src = source_rows(r_ref, cols)
                for b in range(blocks):
                    top = start + 8 * b
                    h = lax.rsqrt(s_ref[top : top + 8, cols])
                    cube = h * h * h
                    whole = h + cube
                    m = s_ref[points + top : points + top + 8, cols] * cube
                    acc[3][b] = added(acc[3][b], m)
                    for k in range(3):
                        acc[k][b] = added(acc[k][b], whole * src[3 + k]) - m * src[k]
            for b in range(blocks):
                top = start + 8 * b
                for k in range(4):
                    sums[top : top + 8, k : k + 1] = jnp.sum(acc[k][b], axis=1, keepdims=True)
        flat = sums[...].T[0:4, :points]
        out_ref[j] = flat[0:3] + own_ref[0:3, :points] * flat[3:4] + wall_ref[j]

    def step(j, s_ref, r_ref, w_ref, own_ref, a_ref):
        center = prepare_own(j, point_ref, density_ref, weight_ref, feature_ref, own_ref, a_ref, 2)
        prepare(j, center, r_ref, w_ref)
        products(a_ref, w_ref, s_ref)

    start_features(feature_ref)
    step(0, s0, r0, w0, o0, a0)

    def body(i, carry):
        j = 2 * i
        step(j + 1, s1, r1, w1, o1, a1)
        evaluate(j, s0, r0, o0)
        step(jnp.minimum(j + 2, cells - 1), s0, r0, w0, o0, a0)
        evaluate(j + 1, s1, r1, o1)
        return carry

    lax.fori_loop(0, cells // 2, body, 0)


def wall_kernel(
    ids_ref,
    patch_ref,
    point_ref,
    density_ref,
    weight_ref,
    out_ref,
    back_ref,
    s0,
    s1,
    r0,
    r1,
    w0,
    w1,
    o0,
    o1,
    a0,
    a1,
    feature_ref,
    sums,
    columns,
):
    cells = out_ref.shape[0]
    points = out_ref.shape[2]
    tiles = r0.shape[1] // lanes
    lane = lax.broadcasted_iota(jnp.int32, (8, lanes), 1)
    back_ref[...] = jnp.zeros_like(back_ref)

    def prepare(j, center, r_ref, w_ref):
        parts = []
        for t in range(tiles):
            left, right = ids_ref[j, 2 * t], ids_ref[j, 2 * t + 1]
            one = pltpu.roll(patch_ref[left // 2], 64 * (left % 2), 1)
            two = pltpu.roll(patch_ref[right // 2], 64 * (1 - right % 2), 1)
            parts.append(jnp.where(lane < 64, one, two) - center)
        raw = jnp.concatenate(parts, axis=1)
        r_ref[...] = raw
        w_ref[...] = source_features(raw)

    def evaluate(j, s_ref, r_ref, own_ref):
        blocks = 2
        columns[...] = own_ref[...].T
        back = [[None] * 4 for _ in range(tiles)]
        for start in range(0, points, 8 * blocks):
            acc = [[None] * blocks for _ in range(4)]
            own = [
                [
                    jnp.broadcast_to(columns[start + 8 * b : start + 8 * b + 8, k : k + 1], (8, lanes))
                    for k in range(6)
                ]
                for b in range(blocks)
            ]
            for c in range(tiles):
                cols = slice(c * lanes, c * lanes + lanes)
                src = source_rows(r_ref, cols)
                for b in range(blocks):
                    top = start + 8 * b
                    h = lax.rsqrt(s_ref[top : top + 8, cols])
                    cube = h * h * h
                    whole = h + cube
                    m = s_ref[points + top : points + top + 8, cols] * cube
                    n = s_ref[2 * points + top : 2 * points + top + 8, cols] * cube
                    acc[3][b] = added(acc[3][b], m)
                    back[c][3] = added(back[c][3], n)
                    for k in range(3):
                        acc[k][b] = added(acc[k][b], whole * src[3 + k]) - m * src[k]
                        back[c][k] = added(back[c][k], whole * own[b][3 + k]) - n * own[b][k]
            for b in range(blocks):
                top = start + 8 * b
                for k in range(4):
                    sums[top : top + 8, k : k + 1] = jnp.sum(acc[k][b], axis=1, keepdims=True)
        flat = sums[...].T[0:4, :points]
        out_ref[j] = flat[0:3] + own_ref[0:3, :points] * flat[3:4]
        for c in range(tiles):
            rows = [jnp.sum(back[c][k], axis=0, keepdims=True) for k in range(4)]
            rows = jnp.concatenate(rows + [jnp.zeros((4, lanes), f32)], axis=0)
            term = rows + r_ref[:, c * lanes : c * lanes + lanes] * rows[3:4, :]
            for half in range(2):
                patch = ids_ref[j, 2 * c + half]
                odd = patch % 2
                moved = pltpu.roll(term, 64 * (odd if half == 0 else 1 - odd), 1)
                kept = jnp.where((lane >= 64) == (odd == 1), moved, 0.0)
                back_ref[patch // 2] += kept

    def step(j, s_ref, r_ref, w_ref, own_ref, a_ref):
        center = prepare_own(j, point_ref, density_ref, weight_ref, feature_ref, own_ref, a_ref, 3)
        prepare(j, center, r_ref, w_ref)
        products(a_ref, w_ref, s_ref)

    start_features(feature_ref)
    own_ref_rows = jnp.zeros_like(o0)
    o0[...] = own_ref_rows
    o1[...] = own_ref_rows
    step(0, s0, r0, w0, o0, a0)

    def body(i, carry):
        j = 2 * i
        step(j + 1, s1, r1, w1, o1, a1)
        evaluate(j, s0, r0, o0)
        step(jnp.minimum(j + 2, cells - 1), s0, r0, w0, o0, a0)
        evaluate(j + 1, s1, r1, o1)
        return carry

    lax.fori_loop(0, cells // 2, body, 0)


def scratch(points, kinds, tiles):
    wide = -(-points // lanes) * lanes
    return [
        pltpu.VMEM((kinds * points, tiles * lanes), f32),
        pltpu.VMEM((kinds * points, tiles * lanes), f32),
        pltpu.VMEM((8, tiles * lanes), f32),
        pltpu.VMEM((8, tiles * lanes), f32),
        pltpu.VMEM((depth, tiles * lanes), bf16),
        pltpu.VMEM((depth, tiles * lanes), bf16),
        pltpu.VMEM((8, wide), f32),
        pltpu.VMEM((8, wide), f32),
        pltpu.VMEM((kinds * points, depth), bf16),
        pltpu.VMEM((kinds * points, depth), bf16),
        pltpu.VMEM((kinds * depth, wide), f32),
        pltpu.VMEM((wide, lanes), f32),
    ]


def local(
    cell_points,
    cell_density,
    cell_weights,
    near_device,
    near_slot,
    near_wall,
    wall_points,
    wall_density,
    wall_weights,
):
    wall_count = lax.axis_size("wall")
    wall_index = lax.axis_index("wall")
    cells, _, points = cell_points.shape
    patch_dev, _, patch_pts = wall_points.shape
    quarter = points // wall_count
    extra = quarter - lanes
    part = patch_pts // wall_count
    wide = -(-points // lanes) * lanes
    vmem = pl.BlockSpec(memory_space=pltpu.VMEM)
    smem = pl.BlockSpec(memory_space=pltpu.SMEM)
    params = pltpu.CompilerParams(vmem_limit_bytes=60 * 2**20)

    cell_load = cell_density * cell_weights[:, None, :]
    raw = jnp.concatenate([2.0 * cell_points, cell_load], axis=1)
    mine = lax.dynamic_slice_in_dim(raw, wall_index * quarter, quarter, 2)
    gap = jnp.zeros((cells, lanes - 6 * extra), f32)
    ends = [mine[:, q, lanes:] for q in range(6)]
    tail = jnp.concatenate([ends[0], gap] + ends[:0:-1], axis=1)[:, None, :]
    block = jnp.concatenate([mine[:, :, :lanes], tail, jnp.zeros((cells, 1, lanes), f32)], axis=1)
    gathered = lax.all_gather(block, "cell", axis=0, tiled=True)

    wall_raw = jnp.concatenate(
        [2.0 * wall_points, wall_density * wall_weights[:, None, :], jnp.zeros((patch_dev, 2, patch_pts), f32)],
        axis=1,
    )
    wall_raw = wall_raw.reshape(patch_dev // 2, 2, 8, wall_count, part).transpose(3, 0, 2, 1, 4)
    wall_raw = wall_raw.reshape(wall_count * (patch_dev // 2), 8, 2 * part)
    patches = lax.all_to_all(wall_raw, "wall", split_axis=0, concat_axis=0, tiled=True)

    tiles = near_wall.shape[1] * part // lanes
    wall_term, back = pl.pallas_call(
        wall_kernel,
        out_shape=(
            jax.ShapeDtypeStruct((cells, 3, points), f32),
            jax.ShapeDtypeStruct(patches.shape, f32),
        ),
        in_specs=[smem] + [vmem] * 4,
        out_specs=(vmem, vmem),
        scratch_shapes=scratch(points, 3, tiles) + [pltpu.VMEM((wide, 8), f32)],
        compiler_params=params,
        cost_estimate=pl.CostEstimate(flops=10**9, bytes_accessed=10**8, transcendentals=0),
        name="wall_pairs",
    )(near_wall, patches, cell_points, cell_density, cell_weights)

    near_ids = near_device * cells + near_slot
    tiles = near_device.shape[1] + 1
    total = pl.pallas_call(
        near_kernel,
        out_shape=jax.ShapeDtypeStruct((cells, 3, points), f32),
        in_specs=[smem] + [vmem] * 5,
        out_specs=vmem,
        scratch_shapes=scratch(points, 2, tiles),
        compiler_params=params,
        cost_estimate=pl.CostEstimate(flops=10**9, bytes_accessed=10**8, transcendentals=0),
        name="near_pairs",
    )(near_ids, gathered, cell_points, cell_density, cell_weights, wall_term)

    total = total.reshape(cells, 3, wall_count, quarter).transpose(2, 0, 1, 3)
    share = jnp.sum(lax.all_to_all(total, "wall", split_axis=0, concat_axis=0, tiled=True), axis=0)
    own = lax.dynamic_slice_in_dim(cell_density, wall_index * quarter, quarter, 2)
    velocity = 0.5 * own + two_stokes_factor * share

    back = lax.all_to_all(back[:, :3, :], "wall", split_axis=0, concat_axis=0, tiled=True)
    back = back.reshape(wall_count, patch_dev // 2, 3, 2, part).transpose(1, 3, 2, 0, 4)
    wall_velocity = 0.5 * wall_density + two_stokes_factor * back.reshape(patch_dev, 3, patch_pts)
    return (velocity, wall_velocity)


def solution(mesh):
    in_specs = (
        P("cell", None, None),
        P("cell", None, None),
        P("cell", None),
        P("cell", None),
        P("cell", None),
        P("cell", None),
        P(("cell", "wall"), None, None),
        P(("cell", "wall"), None, None),
        P(("cell", "wall"), None),
    )
    out_specs = (P("cell", None, "wall"), P(("cell", "wall"), None, None))
    return jax.shard_map(local, mesh=mesh, in_specs=in_specs, out_specs=out_specs, check_vma=False)
```

profile of v0, /device:TPU:1, one launch (start us, length us, event | category | flops | bytes accessed | tf_op | source)
XLA Modules:
  0.0 202.3 jit_solution(8008706809697545702)
XLA Ops:
  7.2 1.1 broadcast_multiply_fusion.1
  8.8 0.7 maximum_maximum_fusion.1
  9.6 1.1 broadcast_multiply_fusion.3
  10.9 0.5 reshape.21
  11.4 0.5 copy.73
  11.9 1.4 reshape.22
  13.3 4.8 %all-to-all-start = ((f32[128,8,128]{2,1,0:T(8,128)}), f32[128,8,128]{2,1,0:T(8,128)S(1)}, u32[]{:S(2)}, u32[]{:S(2)}) async-start(f32[128,8,128]{2,1,0:T(8,128)} %reshape.22), calls=%async_computation | async-start | bytes 1048576 | tf_op jit(solution)/shard_map/all_to_all | solution.py:333
  18.2 0.9 copy.65.point_ref
  19.1 0.9 copy.66.density_ref
  20.0 0.7 copy.62.ids_ref
  20.8 5.6 %all-to-all-done.patch_ref = f32[128,8,128]{2,1,0:T(8,128)S(1)} async-done(((f32[128,8,128]{2,1,0:T(8,128)}), f32[128,8,128]{2,1,0:T(8,128)S(1)}, u32[]{:S(2)}, u32[]{:S(2)}) %all-to-all-start) | async-done | bytes 524320 | tf_op jit(solution)/shard_map/all_to_all | solution.py:333
  26.4 0.8 copy-done.3
  27.2 72.9 %wall_pairs.1 = (f32[32,3,544]{2,1,0:T(4,128)}, f32[128,8,128]{2,1,0:T(8,128)}) custom-call(s32[32,8]{1,0:T(8,128)} %copy.62.ids_ref, f32[128,8,128]{2,1,0:T(8,128)} %copy-done.3, f32[32,3,544]{2,1,0:T(4,128)} %copy.65.point_ref, f32[32,3,544]{2,1,0:T(4,128)} %copy.66.density_ref, f32[32,544]{1,0:T(8,128)} %weight_ref.3), custom_call_target="tpu_custom_call" | custom-call | flops 1000000000 | bytes 100000000 | tf_op jit(solution)/shard_map/wall_pairs/pallas_call | solution.py:336
  100.2 1.8 slice.31
  101.9 3.6 %all-to-all-start.2 = ((f32[128,3,128]{2,1,0:T(4,128)}), f32[128,3,128]{2,1,0:T(4,128)S(1)}, u32[]{:S(2)}, u32[]{:S(2)}) async-start(f32[128,3,128]{2,1,0:T(4,128)} %slice.31), calls=%async_computation.2 | async-start | bytes 524288 | tf_op jit(solution)/shard_map/all_to_all | solution.py:368
  105.5 0.6 multiply_add_fusion.2.ids_ref
  106.2 4.7 %all-to-all-done.2 = f32[128,3,128]{2,1,0:T(4,128)S(1)} async-done(((f32[128,3,128]{2,1,0:T(4,128)}), f32[128,3,128]{2,1,0:T(4,128)S(1)}, u32[]{:S(2)}, u32[]{:S(2)}) %all-to-all-start.2) | async-done | bytes 196640 | tf_op jit(solution)/shard_map/all_to_all | solution.py:368
  111.8 71.1 %near_pairs.1 = f32[32,3,544]{2,1,0:T(4,128)} custom-call(s32[32,8]{1,0:T(8,128)} %multiply_add_fusion.2.ids_ref, f32[1024,8,128]{2,1,0:T(8,128)} %all-gather.2.cloned.1.call-done.gathered_ref, f32[32,3,544]{2,1,0:T(4,128)} %copy.65.point_ref, f32[32,3,544]{2,1,0:T(4,128)} %copy.66.density_ref, f32[32,544]{1,0:T(8,128)} %weight_ref.3, ...), custom_call_target="tpu_custom_call" | custom-call | flops 1000000000 | bytes 100000000 | tf_op jit(solution)/shard_map/near_pairs/pallas_call | solution.py:352
  182.8 1.0 copy.67
  184.2 0.8 copy.68
  185.0 3.5 %all-to-all-start.1 = ((f32[4,32,3,136]{3,1,2,0:T(8,128)}), f32[4,32,3,136]{3,1,2,0:T(8,128)S(1)}, u32[]{:S(2)}, u32[]{:S(2)}) async-start(f32[4,32,3,136]{3,1,2,0:T(8,128)} %copy.68), calls=%async_computation.1 | async-start | bytes 786432 | tf_op jit(solution)/shard_map/all_to_all | solution.py:364
  188.5 0.7 multiply_add_fusion
  189.2 5.5 %all-to-all-done.1 = f32[4,32,3,136]{3,1,2,0:T(8,128)S(1)} async-done(((f32[4,32,3,136]{3,1,2,0:T(8,128)}), f32[4,32,3,136]{3,1,2,0:T(8,128)S(1)}, u32[]{:S(2)}, u32[]{:S(2)}) %all-to-all-start.1) | async-done | bytes 208928 | tf_op jit(solution)/shard_map/all_to_all | solution.py:364
  194.7 0.7 multiply_add_fusion.1
  (35 shorter events, 2.0 us)
Async XLA Ops:
  7.2 104.6 %all-gather.2.cloned.1.call-start = ((), (), s32[]{:S(2)}) async-start(), calls=%async_computation.3 | async-start | bytes 4325376 | tf_op jit(solution)/shard_map/all_gather | solution.py:325
  8.8 9.4 %copy-start.1 = (f32[32,3,544]{2,0,1:T(8,128)S(1)}, f32[32,3,544]{2,0,1:T(8,128)}, u32[]{:S(2)}) copy-start(f32[32,3,544]{2,0,1:T(8,128)} %param.9) | copy-start | bytes 626692
  9.6 9.4 %copy-start = (f32[32,3,544]{2,0,1:T(8,128)S(1)}, f32[32,3,544]{2,0,1:T(8,128)}, u32[]{:S(2)}) copy-start(f32[32,3,544]{2,0,1:T(8,128)} %param.10) | copy-start | bytes 626692
  10.8 9.2 %copy-start.4 = (s32[32,8]{0,1:T(8,128)S(1)}, s32[32,8]{0,1:T(8,128)}, u32[]{:S(2)}) copy-start(s32[32,8]{0,1:T(8,128)} %param.14) | copy-start | bytes 3076
  10.8 9.9 %copy-start.5 = (s32[32,8]{0,1:T(8,128)S(1)}, s32[32,8]{0,1:T(8,128)}, u32[]{:S(2)}) copy-start(s32[32,8]{0,1:T(8,128)} %param.12) | copy-start | bytes 3076
  10.8 9.9 %copy-start.6 = (s32[32,8]{0,1:T(8,128)S(1)}, s32[32,8]{0,1:T(8,128)}, u32[]{:S(2)}) copy-start(s32[32,8]{0,1:T(8,128)} %param.13) | copy-start | bytes 3076
  13.3 13.1 %all-to-all-start = ((f32[128,8,128]{2,1,0:T(8,128)}), f32[128,8,128]{2,1,0:T(8,128)S(1)}, u32[]{:S(2)}, u32[]{:S(2)}) async-start(f32[128,8,128]{2,1,0:T(8,128)} %reshape.22), calls=%async_computation | async-start | bytes 1048576 | tf_op jit(solution)/shard_map/all_to_all | solution.py:333
  26.4 0.8 copy-start.3
  101.9 8.9 %all-to-all-start.2 = ((f32[128,3,128]{2,1,0:T(4,128)}), f32[128,3,128]{2,1,0:T(4,128)S(1)}, u32[]{:S(2)}, u32[]{:S(2)}) async-start(f32[128,3,128]{2,1,0:T(4,128)} %slice.31), calls=%async_computation.2 | async-start | bytes 524288 | tf_op jit(solution)/shard_map/all_to_all | solution.py:368
  111.8 76.7 %copy-start.2 = (f32[64,3,256]{2,0,1:T(8,128)S(1)}, f32[64,3,256]{2,0,1:T(8,128)}, u32[]{:S(2)}) copy-start(f32[64,3,256]{2,0,1:T(8,128)} %param.16) | copy-start | bytes 589828
  185.0 9.7 %all-to-all-start.1 = ((f32[4,32,3,136]{3,1,2,0:T(8,128)}), f32[4,32,3,136]{3,1,2,0:T(8,128)S(1)}, u32[]{:S(2)}, u32[]{:S(2)}) async-start(f32[4,32,3,136]{3,1,2,0:T(8,128)} %copy.68), calls=%async_computation.1 | async-start | bytes 786432 | tf_op jit(solution)/shard_map/all_to_all | solution.py:364
Sparse Core Ops, SparseCore 0:
  10.8 50.0 all-gather.1
where the time goes:
time: 206 us; the launch traced here: 202 us
  Pallas kernels  144 us (70%)
  waiting for transfers between devices  15.8 us (8%)
  between operations  14.2 us (7%)
  starting transfers between devices  11.9 us (6%)
  local copies, waits for them, and re-layouts  10.9 us (5%)
  other arithmetic  5.4 us (3%)
    pallas_call x1, Pallas kernels, local(): pl.pallas_call(wall_kernel, out_shape=(jax.ShapeDtypeStruct((cells, 3, po...  72.9 us
    pallas_call x1, Pallas kernels, local(): pl.pallas_call(near_kernel, out_shape=jax.ShapeDtypeStruct((cells, 3, poi...  71.1 us
    all_to_all x1, waiting for transfers between devices, local(): lax.all_to_all(wall_raw, 'wall', split_axis=0, concat_axis=0, tiled=True)  5.62 us
    all_to_all x1, waiting for transfers between devices, local(): lax.all_to_all(total, 'wall', split_axis=0, concat_axis=0, tiled=True)  5.48 us
    all_to_all x1, starting transfers between devices, local(): lax.all_to_all(wall_raw, 'wall', split_axis=0, concat_axis=0, tiled=True)  4.84 us
    all_to_all x1, waiting for transfers between devices, local(): lax.all_to_all(back[:, :3, :], 'wall', split_axis=0, concat_axis=0, tiled...  4.7 us
  transfers between devices with their start and end apart: 4, of which 3 were waited for; matrix products, arithmetic and copies ran while one was open for 5% of the time, Pallas kernels for 36%

commit v1 on v0

v1 whole, which is shorter than its diff:
```python
import jax
import jax.numpy as jnp
from jax import lax
from jax.experimental import pallas as pl
from jax.experimental.pallas import tpu as pltpu
from jax.sharding import PartitionSpec as P

f32 = jnp.float32
bf16 = jnp.bfloat16
two_stokes_factor = 2.0 * 0.039788735772973836
levels = ((1, 1), (1, 2), (1, 3), (2, 1), (2, 2), (3, 1))
depth = 64
lanes = 128


def split3(x):
    first = x.astype(bf16).astype(f32)
    rest = x - first
    second = rest.astype(bf16).astype(f32)
    return first, second, rest - second


def source_features(raw):
    y = [raw[i : i + 1, :] for i in range(3)]
    g = [raw[i : i + 1, :] for i in range(3, 6)]
    square = y[0] * y[0] + y[1] * y[1] + y[2] * y[2] + 1.0
    dot = g[0] * y[0] + g[1] * y[1] + g[2] * y[2]
    rows = jnp.concatenate(
        [-2.0 * y[0], -2.0 * y[1], -2.0 * y[2], square, g[0], g[1], g[2], -dot], axis=0
    )
    parts = split3(rows)
    one = jnp.ones_like(rows)
    stack = [parts[p - 1] for p, _ in levels] + [one, jnp.zeros_like(rows)]
    return jnp.concatenate(stack, axis=0).astype(bf16)


def own_kernel(point_ref, density_ref, weight_ref, target_ref, own_ref, center_ref, feature_ref):
    points = point_ref.shape[2]
    first = pl.program_id(0) * point_ref.shape[0]
    start_features(feature_ref)

    def cell(i, carry):
        x = 2.0 * point_ref[i]
        center = jnp.sum(x, axis=1, keepdims=True) * (1.0 / points)
        x = x - center
        load = density_ref[i] * weight_ref[pl.ds(first + i, 1), :]
        own_ref[i] = jnp.zeros(own_ref.shape[1:], f32)
        own_ref[i, 0:3, :points] = x
        own_ref[i, 3:6, :points] = load
        xs, ls = split3(x), split3(-0.5 * load)
        squares = split3(jnp.sum(x * x, axis=0, keepdims=True))
        dots = split3(-jnp.sum(x * load, axis=0, keepdims=True))
        for n, (_, q) in enumerate(levels):
            feature_ref[8 * n : 8 * n + 3, :points] = xs[q - 1]
            feature_ref[depth + 8 * n + 4 : depth + 8 * n + 7, :points] = xs[q - 1]
            feature_ref[2 * depth + 8 * n : 2 * depth + 8 * n + 3, :points] = ls[q - 1]
        for n in range(3):
            feature_ref[48 + n : 49 + n, :points] = squares[n]
            feature_ref[2 * depth + 48 + n : 2 * depth + 49 + n, :points] = dots[n]
        for kind in range(3):
            turned = feature_ref[kind * depth : kind * depth + depth, :].T
            target_ref[i, kind * points : kind * points + points, :] = turned[:points].astype(bf16)
        center_ref[i] = jnp.concatenate(
            [jnp.broadcast_to(center, (3, lanes)), jnp.zeros((5, lanes), f32)], axis=0
        )
        return carry

    lax.fori_loop(0, point_ref.shape[0], cell, 0)


def start_features(feature_ref):
    feature_ref[...] = jnp.zeros_like(feature_ref)
    one = jnp.ones((1, feature_ref.shape[1]), f32)
    for i, (_, q) in enumerate(levels):
        if q == 1:
            feature_ref[8 * i + 3 : 8 * i + 4, :] = one
            feature_ref[depth + 8 * i + 7 : depth + 8 * i + 8, :] = one


def product_tiles(a_ref, w_ref, s_ref):
    n = w_ref.shape[1]

    def tile(c):
        e = min(n, c + 256)
        s_ref[:, c:e] = jnp.dot(a_ref[...], w_ref[:, c:e], preferred_element_type=f32)

    return [lambda c=c: tile(c) for c in range(0, n, 256)]


def source_rows(r_ref, cols):
    return [jnp.broadcast_to(r_ref[i : i + 1, cols], (8, lanes)) for i in range(6)]


def added(total, term):
    return term if total is None else total + term


def woven(main, side):
    done = 0
    for i, piece in enumerate(main):
        while done < len(side) and done * len(main) <= i * len(side):
            side[done]()
            done += 1
        piece()
    for piece in side[done:]:
        piece()


def keep_sums(acc, top, acc_ref):
    for k in range(4):
        rows = jnp.concatenate(acc[k], axis=0)
        high = rows.astype(bf16)
        low = (rows - high.astype(f32)).astype(bf16)
        acc_ref[top : top + rows.shape[0], 2 * k * lanes : (2 * k + 1) * lanes] = high
        acc_ref[top : top + rows.shape[0], (2 * k + 1) * lanes : (2 * k + 2) * lanes] = low


def finish_pieces(j, acc_ref, own_ref, fold_ref, out_ref, more_ref):
    points = out_ref.shape[2]

    def fold():
        flat = lax.dot_general(
            fold_ref[...], acc_ref[...], (((1,), (1,)), ((), ())), preferred_element_type=f32
        )
        total = flat[0:3] + own_ref[j, 0:3, :points] * flat[3:4]
        out_ref[j] = total if more_ref is None else total + more_ref[j]

    return [fold]


def start_fold(fold_ref):
    row = lax.broadcasted_iota(jnp.int32, fold_ref.shape, 0)
    column = lax.broadcasted_iota(jnp.int32, fold_ref.shape, 1)
    fold_ref[...] = jnp.where(row == column // (2 * lanes), 1.0, 0.0).astype(bf16)


def near_kernel(
    ids_ref,
    gathered_ref,
    own_ref,
    center_ref,
    target_ref,
    wall_ref,
    out_ref,
    s0,
    s1,
    r0,
    r1,
    w0,
    w1,
    a0,
    a1,
    c0,
    c1,
    fold_ref,
    copied,
):
    cells = out_ref.shape[0]
    points = out_ref.shape[2]
    tiles = r0.shape[1] // lanes
    blocks = 4

    def prepare(j, r_ref, w_ref):
        center = center_ref[j]
        lane = lax.broadcasted_iota(jnp.int32, (8, lanes), 1)
        tail = jnp.zeros((8, lanes), f32)
        parts = []
        for k in range(8):
            block = gathered_ref[ids_ref[j, k]]
            parts.append(block - center)
            last = jnp.broadcast_to(block[6:7, :], (8, lanes))
            last = pltpu.roll(last, 8 * k, 1, stride=8, stride_axis=0)
            tail = jnp.where((lane >= 8 * k) & (lane < 8 * k + 8), last, tail)
        parts.append(jnp.where(lane < 64, tail - center, 0.0))
        raw = jnp.concatenate(parts, axis=1)
        r_ref[...] = raw
        w_ref[...] = source_features(raw)

    def chunk(start, s_ref, r_ref, acc_ref):
        acc = [[None] * blocks for _ in range(4)]
        for c in range(tiles):
            cols = slice(c * lanes, c * lanes + lanes)
            src = source_rows(r_ref, cols)
            for b in range(blocks):
                top = start + 8 * b
                h = lax.rsqrt(s_ref[top : top + 8, cols])
                cube = h * h * h
                whole = h + cube
                m = s_ref[points + top : points + top + 8, cols] * cube
                acc[3][b] = added(acc[3][b], m)
                for k in range(3):
                    acc[k][b] = added(acc[k][b], whole * src[3 + k]) - m * src[k]
        keep_sums(acc, start, acc_ref)

    def fetch(j, slot):
        a_ref = (a0, a1)[slot]
        source = target_ref.at[jnp.minimum(j, cells - 1), pl.ds(0, a_ref.shape[0])]
        return pltpu.make_async_copy(source, a_ref, copied.at[slot])

    def stage(j, slot, last):
        s_ref, r_ref, w_ref, a_ref, acc_ref = sets[slot]
        next_s, next_r, next_w, next_a, next_acc = sets[1 - slot]
        fetch(j + 2, slot).start()
        fetch(j + 1, 1 - slot).wait()
        side = finish_pieces(jnp.maximum(j - 1, 0), next_acc, own_ref, fold_ref, out_ref, wall_ref)
        side += [lambda: prepare(last, next_r, next_w)]
        side += product_tiles(next_a, next_w, next_s)
        main = [lambda t=t: chunk(t, s_ref, r_ref, acc_ref) for t in range(0, points, 8 * blocks)]
        woven(main, side)

    sets = ((s0, r0, w0, a0, c0), (s1, r1, w1, a1, c1))
    start_fold(fold_ref)
    c1[...] = jnp.zeros_like(c1)
    fetch(0, 0).start()
    fetch(1, 1).start()
    prepare(0, r0, w0)
    fetch(0, 0).wait()
    for piece in product_tiles(a0, w0, s0):
        piece()

    def body(i, carry):
        j = 2 * i
        stage(j, 0, j + 1)
        stage(j + 1, 1, jnp.minimum(j + 2, cells - 1))
        return carry

    lax.fori_loop(0, cells // 2, body, 0)
    fetch(cells + 1, 1).wait()
    for piece in finish_pieces(cells - 1, c1, own_ref, fold_ref, out_ref, wall_ref):
        piece()


def wall_kernel(
    ids_ref,
    patch_ref,
    own_ref,
    center_ref,
    target_ref,
    out_ref,
    back_ref,
    s0,
    s1,
    r0,
    r1,
    w0,
    w1,
    a0,
    a1,
    c0,
    c1,
    fold_ref,
    copied,
    p0,
    p1,
    pick_ref,
):
    cells = out_ref.shape[0]
    points = out_ref.shape[2]
    tiles = r0.shape[1] // lanes
    blocks = 2
    lane = lax.broadcasted_iota(jnp.int32, (8, lanes), 1)

    def prepare(j, r_ref, w_ref):
        center = center_ref[j]
        parts = []
        for t in range(tiles):
            left, right = ids_ref[j, 2 * t], ids_ref[j, 2 * t + 1]
            one = pltpu.roll(patch_ref[left // 2], 64 * (left % 2), 1)
            two = pltpu.roll(patch_ref[right // 2], 64 * (1 - right % 2), 1)
            parts.append(jnp.where(lane < 64, one, two) - center)
        raw = jnp.concatenate(parts, axis=1)
        r_ref[...] = raw
        w_ref[...] = source_features(raw)

    def chunk(start, s_ref, r_ref, acc_ref, p_ref, back):
        acc = [[None] * blocks for _ in range(4)]
        own = [
            [p_ref[start + 8 * b : start + 8 * b + 8, k * lanes : k * lanes + lanes] for k in range(6)]
            for b in range(blocks)
        ]
        for c in range(tiles):
            cols = slice(c * lanes, c * lanes + lanes)
            src = source_rows(r_ref, cols)
            for b in range(blocks):
                top = start + 8 * b
                h = lax.rsqrt(s_ref[top : top + 8, cols])
                cube = h * h * h
                whole = h + cube
                m = s_ref[points + top : points + top + 8, cols] * cube
                n = s_ref[2 * points + top : 2 * points + top + 8, cols] * cube
                acc[3][b] = added(acc[3][b], m)
                back[c][3] = added(back[c][3], n)
                for k in range(3):
                    acc[k][b] = added(acc[k][b], whole * src[3 + k]) - m * src[k]
                    back[c][k] = added(back[c][k], whole * own[b][3 + k]) - n * own[b][k]
        keep_sums(acc, start, acc_ref)

    def give_back(j, r_ref, back):
        for c in range(tiles):
            rows = [jnp.sum(back[c][k], axis=0, keepdims=True) for k in range(4)]
            rows = jnp.concatenate(rows + [jnp.zeros((4, lanes), f32)], axis=0)
            term = rows + r_ref[:, c * lanes : c * lanes + lanes] * rows[3:4, :]
            for half in range(2):
                patch = ids_ref[j, 2 * c + half]
                odd = patch % 2
                moved = pltpu.roll(term, 64 * (odd if half == 0 else 1 - odd), 1)
                kept = jnp.where((lane >= 64) == (odd == 1), moved, 0.0)
                back_ref[patch // 2] += kept

    def fetch(j, slot):
        a_ref = (a0, a1)[slot]
        source = target_ref.at[jnp.minimum(j, cells - 1), pl.ds(0, a_ref.shape[0])]
        return pltpu.make_async_copy(source, a_ref, copied.at[slot])

    def spread_pieces(a_ref, p_ref):
        half = 3 * lanes

        def positions():
            p_ref[:, :half] = jnp.dot(a_ref[:points], pick_ref[:, :half], preferred_element_type=f32)

        def loads():
            p_ref[:, half:] = jnp.dot(a_ref[2 * points :], pick_ref[:, half:], preferred_element_type=f32)

        return [positions, loads]

    def stage(j, slot, last):
        s_ref, r_ref, w_ref, a_ref, acc_ref, p_ref = sets[slot]
        next_s, next_r, next_w, next_a, next_acc, next_p = sets[1 - slot]
        fetch(j + 2, slot).start()
        fetch(j + 1, 1 - slot).wait()
        side = finish_pieces(jnp.maximum(j - 1, 0), next_acc, own_ref, fold_ref, out_ref, None)
        side += [lambda: prepare(last, next_r, next_w)]
        side += product_tiles(next_a, next_w, next_s) + spread_pieces(next_a, next_p)
        back = [[None] * 4 for _ in range(tiles)]
        main = [lambda t=t: chunk(t, s_ref, r_ref, acc_ref, p_ref, back) for t in range(0, points, 8 * blocks)]
        woven(main, side)
        give_back(j, r_ref, back)

    sets = ((s0, r0, w0, a0, c0, p0), (s1, r1, w1, a1, c1, p1))
    back_ref[...] = jnp.zeros_like(back_ref)
    start_fold(fold_ref)
    feature = lax.broadcasted_iota(jnp.int32, pick_ref.shape, 0)
    column = lax.broadcasted_iota(jnp.int32, pick_ref.shape, 1) // lanes
    hit = (feature < 24) & (feature % 8 == column % 3)
    pick_ref[...] = jnp.where(hit, jnp.where(column < 3, 1.0, -2.0), 0.0).astype(bf16)
    c1[...] = jnp.zeros_like(c1)
    fetch(0, 0).start()
    fetch(1, 1).start()
    prepare(0, r0, w0)
    fetch(0, 0).wait()
    for piece in product_tiles(a0, w0, s0) + spread_pieces(a0, p0):
        piece()

    def body(i, carry):
        j = 2 * i
        stage(j, 0, j + 1)
        stage(j + 1, 1, jnp.minimum(j + 2, cells - 1))
        return carry

    lax.fori_loop(0, cells // 2, body, 0)
    fetch(cells + 1, 1).wait()
    for piece in finish_pieces(cells - 1, c1, own_ref, fold_ref, out_ref, None):
        piece()


def scratch(points, kinds, tiles):
    pairs = [
        pltpu.VMEM((kinds * points, tiles * lanes), f32),
        pltpu.VMEM((8, tiles * lanes), f32),
        pltpu.VMEM((depth, tiles * lanes), bf16),
        pltpu.VMEM((kinds * points, depth), bf16),
        pltpu.VMEM((points, 8 * lanes), bf16),
    ]
    shapes = [shape for shape in pairs for _ in range(2)]
    shapes += [pltpu.VMEM((16, 8 * lanes), bf16), pltpu.SemaphoreType.DMA((2,))]
    if kinds == 3:
        shapes += [pltpu.VMEM((points, 6 * lanes), f32)] * 2 + [pltpu.VMEM((depth, 6 * lanes), bf16)]
    return shapes


def local(
    cell_points,
    cell_density,
    cell_weights,
    near_device,
    near_slot,
    near_wall,
    wall_points,
    wall_density,
    wall_weights,
):
    wall_count = lax.axis_size("wall")
    wall_index = lax.axis_index("wall")
    cells, _, points = cell_points.shape
    patch_dev, _, patch_pts = wall_points.shape
    quarter = points // wall_count
    extra = quarter - lanes
    part = patch_pts // wall_count
    vmem = pl.BlockSpec(memory_space=pltpu.VMEM)
    smem = pl.BlockSpec(memory_space=pltpu.SMEM)
    hbm = pl.BlockSpec(memory_space=pl.ANY)
    params = pltpu.CompilerParams(vmem_limit_bytes=60 * 2**20)

    cell_load = cell_density * cell_weights[:, None, :]
    raw = jnp.concatenate([2.0 * cell_points, cell_load], axis=1)
    mine = lax.dynamic_slice_in_dim(raw, wall_index * quarter, quarter, 2)
    gap = jnp.zeros((cells, lanes - 6 * extra), f32)
    ends = [mine[:, q, lanes:] for q in range(6)]
    tail = jnp.concatenate([ends[0], gap] + ends[:0:-1], axis=1)[:, None, :]
    block = jnp.concatenate([mine[:, :, :lanes], tail, jnp.zeros((cells, 1, lanes), f32)], axis=1)
    gathered = lax.all_gather(block, "cell", axis=0, tiled=True)

    wall_raw = jnp.concatenate(
        [2.0 * wall_points, wall_density * wall_weights[:, None, :], jnp.zeros((patch_dev, 2, patch_pts), f32)],
        axis=1,
    )
    wall_raw = wall_raw.reshape(patch_dev // 2, 2, 8, wall_count, part).transpose(3, 0, 2, 1, 4)
    wall_raw = wall_raw.reshape(wall_count * (patch_dev // 2), 8, 2 * part)
    patches = lax.all_to_all(wall_raw, "wall", split_axis=0, concat_axis=0, tiled=True)

    wide = -(-points // lanes) * lanes
    batch = 4

    def by_batch(*shape):
        return pl.BlockSpec((batch,) + shape, lambda i: (i, 0, 0))

    target, own_rows, center = pl.pallas_call(
        own_kernel,
        grid=(cells // batch,),
        out_shape=(
            jax.ShapeDtypeStruct((cells, 3 * points, depth), bf16),
            jax.ShapeDtypeStruct((cells, 8, wide), f32),
            jax.ShapeDtypeStruct((cells, 8, lanes), f32),
        ),
        in_specs=[by_batch(3, points), by_batch(3, points), vmem],
        out_specs=(by_batch(3 * points, depth), by_batch(8, wide), by_batch(8, lanes)),
        scratch_shapes=[pltpu.VMEM((3 * depth, wide), f32)],
        compiler_params=pltpu.CompilerParams(vmem_limit_bytes=24 * 2**20),
        cost_estimate=pl.CostEstimate(flops=10**7, bytes_accessed=2 * 10**7, transcendentals=0),
        name="own_features",
    )(cell_points, cell_density, cell_weights)

    tiles = near_wall.shape[1] * part // lanes
    wall_term, back = pl.pallas_call(
        wall_kernel,
        out_shape=(
            jax.ShapeDtypeStruct((cells, 3, points), f32),
            jax.ShapeDtypeStruct(patches.shape, f32),
        ),
        in_specs=[smem] + [vmem] * 3 + [hbm],
        out_specs=(vmem, vmem),
        scratch_shapes=scratch(points, 3, tiles),
        compiler_params=params,
        cost_estimate=pl.CostEstimate(flops=10**9, bytes_accessed=10**8, transcendentals=0),
        name="wall_pairs",
    )(near_wall, patches, own_rows, center, target)

    near_ids = near_device * cells + near_slot
    tiles = near_device.shape[1] + 1
    total = pl.pallas_call(
        near_kernel,
        out_shape=jax.ShapeDtypeStruct((cells, 3, points), f32),
        in_specs=[smem] + [vmem] * 3 + [hbm, vmem],
        out_specs=vmem,
        scratch_shapes=scratch(points, 2, tiles),
        compiler_params=params,
        cost_estimate=pl.CostEstimate(flops=10**9, bytes_accessed=10**8, transcendentals=0),
        name="near_pairs",
    )(near_ids, gathered, own_rows, center, target, wall_term)

    total = total.reshape(cells, 3, wall_count, quarter).transpose(2, 0, 1, 3)
    share = jnp.sum(lax.all_to_all(total, "wall", split_axis=0, concat_axis=0, tiled=True), axis=0)
    own = lax.dynamic_slice_in_dim(cell_density, wall_index * quarter, quarter, 2)
    velocity = 0.5 * own + two_stokes_factor * share

    back = lax.all_to_all(back[:, :3, :], "wall", split_axis=0, concat_axis=0, tiled=True)
    back = back.reshape(wall_count, patch_dev // 2, 3, 2, part).transpose(1, 3, 2, 0, 4)
    wall_velocity = 0.5 * wall_density + two_stokes_factor * back.reshape(patch_dev, 3, patch_pts)
    return (velocity, wall_velocity)


def solution(mesh):
    in_specs = (
        P("cell", None, None),
        P("cell", None, None),
        P("cell", None),
        P("cell", None),
        P("cell", None),
        P("cell", None),
        P(("cell", "wall"), None, None),
        P(("cell", "wall"), None, None),
        P(("cell", "wall"), None),
    )
    out_specs = (P("cell", None, "wall"), P(("cell", "wall"), None, None))
    return jax.shard_map(local, mesh=mesh, in_specs=in_specs, out_specs=out_specs, check_vma=False)
```

time: 206 us -> 237 us (1.15)
  Pallas kernels: 144 us -> 169 us
  local copies, waits for them, and re-layouts: 10.9 us -> 20.5 us
  waiting for transfers between devices: 15.8 us -> 10.4 us
    pallas_call x1, Pallas kernels: 71.1 us -> 82.6 us  [local(): pl.pallas_call(near_kernel, out_shape=jax.ShapeDtypeStruct((cells, 3, poi...]
    pallas_call x0 -> x1, Pallas kernels: none -> 10.6 us  [local(): pl.pallas_call(own_kernel, grid=(cells // batch,), out_shape=(jax.ShapeDt...]
    unnamed x19 -> x17, local copies, waits for them, and re-layouts: 3.48 us -> 13.1 us
    all_to_all x1, waiting for transfers between devices: 5.62 us -> 0.01 us  [local(): lax.all_to_all(wall_raw, 'wall', split_axis=0, concat_axis=0, tiled=True)]
    pallas_call x1, Pallas kernels: 72.9 us -> 76.1 us  [local(): pl.pallas_call(wall_kernel, out_shape=(jax.ShapeDtypeStruct((cells, 3, po...]
  transfers between devices with their start and end apart: 4 -> 4, of which waited for: 3 -> 2; matrix products, arithmetic and copies ran while one was open for 5% -> 5% of each run, Pallas kernels for 36% -> 37%
where the time goes in v1:
time: 237 us; the launch traced here: 233 us
  Pallas kernels  169 us (71%)
  local copies, waits for them, and re-layouts  20.5 us (9%)
  between operations  14.2 us (6%)
  starting transfers between devices  12.6 us (5%)
  waiting for transfers between devices  10.4 us (4%)
  other arithmetic  6.28 us (3%)
    pallas_call x1, Pallas kernels, local(): pl.pallas_call(near_kernel, out_shape=jax.ShapeDtypeStruct((cells, 3, poi...  82.6 us
    pallas_call x1, Pallas kernels, local(): pl.pallas_call(wall_kernel, out_shape=(jax.ShapeDtypeStruct((cells, 3, po...  76.1 us
    unnamed x17, local copies, waits for them, and re-layouts  13.1 us
    pallas_call x1, Pallas kernels, local(): pl.pallas_call(own_kernel, grid=(cells // batch,), out_shape=(jax.ShapeDt...  10.6 us
    all_to_all x1, waiting for transfers between devices, local(): lax.all_to_all(total, 'wall', split_axis=0, concat_axis=0, tiled=True)  5.48 us
    all_to_all x1, waiting for transfers between devices, local(): lax.all_to_all(back[:, :3, :], 'wall', split_axis=0, concat_axis=0, tiled...  4.92 us
    all_to_all x1, starting transfers between devices, local(): lax.all_to_all(wall_raw, 'wall', split_axis=0, concat_axis=0, tiled=True)  4.84 us
  transfers between devices with their start and end apart: 4, of which 2 were waited for; matrix products, arithmetic and copies ran while one was open for 5% of the time, Pallas kernels for 37%

profile of v1, /device:TPU:1, one launch (start us, length us, event | category | flops | bytes accessed | tf_op | source)
XLA Modules:
  0.0 233.3 jit_solution(7231899407127237686)
XLA Ops:
  7.2 1.1 broadcast_multiply_fusion.1
  9.6 1.1 broadcast_multiply_fusion.3
  11.8 1.4 reshape.22
  13.2 4.8 %all-to-all-start = ((f32[128,8,128]{2,1,0:T(8,128)}), f32[128,8,128]{2,1,0:T(8,128)S(1)}, u32[]{:S(2)}, u32[]{:S(2)}) async-start(f32[128,8,128]{2,1,0:T(8,128)} %reshape.22), calls=%async_computation | async-start | bytes 1048576 | tf_op jit(solution)/shard_map/all_to_all | solution.py:419
  18.1 1.1 copy.53.point_ref
  19.2 1.1 copy.54.density_ref
  20.3 0.8 copy.49
  21.1 0.8 copy.51
  21.8 1.4 copy.56.ids_ref
  23.2 0.9 copy-done.3
  24.1 10.6 %own_features.1 = (bf16[32,1632,64]{2,1,0:T(8,128)(2,1)S(1)}, f32[32,8,640]{2,1,0:T(8,128)S(1)}, f32[32,8,128]{2,1,0:T(8,128)S(1)}) custom-call(f32[32,3,544]{2,1,0:T(4,128)S(1)} %copy.53.point_ref, f32[32,3,544]{2,1,0:T(4,128)S(1)} %copy.54.density_ref, f32[32,544]{1,0:T(8,128)S(1)} %copy-done.3), custom_call_target="tpu_custom_call" | custom-call | flops 10000000 | bytes 20000000 | tf_op jit(solution)/shard_map/own_features/pallas_call | solution.py:427
  34.7 4.8 %copy-done = bf16[32,1632,64]{2,1,0:T(8,128)(2,1)} copy-done((bf16[32,1632,64]{2,1,0:T(8,128)(2,1)}, bf16[32,1632,64]{2,1,0:T(8,128)(2,1)S(1)}, u32[]{:S(2)}) %copy-start) | copy-done | bytes 6684696
  39.5 0.9 copy-done.1
  41.0 0.8 copy-done.4
  41.8 76.1 %wall_pairs.1 = (f32[32,3,544]{2,1,0:T(4,128)}, f32[128,8,128]{2,1,0:T(8,128)}) custom-call(s32[32,8]{1,0:T(8,128)} %copy.56.ids_ref, f32[128,8,128]{2,1,0:T(8,128)} %copy-done.4, f32[32,8,640]{2,1,0:T(8,128)} %copy-done.1, f32[32,8,128]{2,1,0:T(8,128)} %copy-done.2, bf16[32,1632,64]{2,1,0:T(8,128)(2,1)} %copy-done), custom_call_target="tpu_custom_call" | custom-call | flops 1000000000 | bytes 100000000 | tf_op jit(solution)/shard_map/wall_pairs/pallas_call | solution.py:444
  117.9 1.8 slice.31
  119.7 4.2 %all-to-all-start.2 = ((f32[128,3,128]{2,1,0:T(4,128)}), f32[128,3,128]{2,1,0:T(4,128)S(1)}, u32[]{:S(2)}, u32[]{:S(2)}) async-start(f32[128,3,128]{2,1,0:T(4,128)} %slice.31), calls=%async_computation.2 | async-start | bytes 524288 | tf_op jit(solution)/shard_map/all_to_all | solution.py:476
  124.6 4.9 %all-to-all-done.2 = f32[128,3,128]{2,1,0:T(4,128)S(1)} async-done(((f32[128,3,128]{2,1,0:T(4,128)}), f32[128,3,128]{2,1,0:T(4,128)S(1)}, u32[]{:S(2)}, u32[]{:S(2)}) %all-to-all-start.2) | async-done | bytes 196640 | tf_op jit(solution)/shard_map/all_to_all | solution.py:476
  130.4 82.6 %near_pairs.1 = f32[32,3,544]{2,1,0:T(4,128)} custom-call(s32[32,8]{1,0:T(8,128)} %multiply_add_fusion.2.ids_ref, f32[1024,8,128]{2,1,0:T(8,128)} %all-gather.2.cloned.1.call-done.gathered_ref, f32[32,8,640]{2,1,0:T(8,128)} %copy-done.1, f32[32,8,128]{2,1,0:T(8,128)} %copy-done.2, bf16[32,1632,64]{2,1,0:T(8,128)(2,1)} %copy-done, ...), custom_call_target="tpu_custom_call" | custom-call | flops 1000000000 | bytes 100000000 | tf_op jit(solution)/shard_map/near_pairs/pallas_call | solution.py:460
  213.0 1.0 copy.57
  214.3 0.8 copy.58
  215.1 3.5 %all-to-all-start.1 = ((f32[4,32,3,136]{3,1,2,0:T(8,128)}), f32[4,32,3,136]{3,1,2,0:T(8,128)S(1)}, u32[]{:S(2)}, u32[]{:S(2)}) async-start(f32[4,32,3,136]{3,1,2,0:T(8,128)} %copy.58), calls=%async_computation.1 | async-start | bytes 786432 | tf_op jit(solution)/shard_map/all_to_all | solution.py:472
  219.3 5.5 %all-to-all-done.1 = f32[4,32,3,136]{3,1,2,0:T(8,128)S(1)} async-done(((f32[4,32,3,136]{3,1,2,0:T(8,128)}), f32[4,32,3,136]{3,1,2,0:T(8,128)S(1)}, u32[]{:S(2)}, u32[]{:S(2)}) %all-to-all-start.1) | async-done | bytes 208928 | tf_op jit(solution)/shard_map/all_to_all | solution.py:472
  224.8 1.7 multiply_add_fusion.1
  (34 shorter events, 5.5 us)
Async XLA Ops:
  7.2 123.2 %all-gather.2.cloned.1.call-start = ((), (), s32[]{:S(2)}) async-start(), calls=%async_computation.3 | async-start | bytes 4325376 | tf_op jit(solution)/shard_map/all_gather | solution.py:411
  13.2 27.8 %all-to-all-start = ((f32[128,8,128]{2,1,0:T(8,128)}), f32[128,8,128]{2,1,0:T(8,128)S(1)}, u32[]{:S(2)}, u32[]{:S(2)}) async-start(f32[128,8,128]{2,1,0:T(8,128)} %reshape.22), calls=%async_computation | async-start | bytes 1048576 | tf_op jit(solution)/shard_map/all_to_all | solution.py:419
  23.2 0.9 copy-start.3
  34.7 4.8 %copy-start = (bf16[32,1632,64]{2,1,0:T(8,128)(2,1)}, bf16[32,1632,64]{2,1,0:T(8,128)(2,1)S(1)}, u32[]{:S(2)}) copy-start(bf16[32,1632,64]{2,1,0:T(8,128)(2,1)S(1)} %get-tuple-element.9.target_ref) | copy-start | bytes 20054020
  39.5 0.9 copy-start.1
  40.3 0.7 copy-start.2
  41.0 0.8 copy-start.4
  117.9 100.7 %copy-start.5 = (f32[64,3,256]{2,0,1:T(8,128)S(1)}, f32[64,3,256]{2,0,1:T(8,128)}, u32[]{:S(2)}) copy-start(f32[64,3,256]{2,0,1:T(8,128)} %param.16) | copy-start | bytes 589828
  119.7 9.8 %all-to-all-start.2 = ((f32[128,3,128]{2,1,0:T(4,128)}), f32[128,3,128]{2,1,0:T(4,128)S(1)}, u32[]{:S(2)}, u32[]{:S(2)}) async-start(f32[128,3,128]{2,1,0:T(4,128)} %slice.31), calls=%async_computation.2 | async-start | bytes 524288 | tf_op jit(solution)/shard_map/all_to_all | solution.py:476
  215.1 9.7 %all-to-all-start.1 = ((f32[4,32,3,136]{3,1,2,0:T(8,128)}), f32[4,32,3,136]{3,1,2,0:T(8,128)S(1)}, u32[]{:S(2)}, u32[]{:S(2)}) async-start(f32[4,32,3,136]{3,1,2,0:T(8,128)} %copy.58), calls=%async_computation.1 | async-start | bytes 786432 | tf_op jit(solution)/shard_map/all_to_all | solution.py:472
Sparse Core Ops, SparseCore 0:
  10.8 50.1 all-gather.1

commit v2 on v0

--- a/solution.py
+++ b/solution.py
@@ -71,12 +71,15 @@
             feature_ref[depth + 8 * i + 7 : depth + 8 * i + 8, :] = one
 
 
-def products(a_ref, w_ref, s_ref):
+def product_tiles(a_ref, w_ref, s_ref):
     n = w_ref.shape[1]
-    for c in range(0, n, 256):
+
+    def tile(c):
         e = min(n, c + 256)
         s_ref[:, c:e] = jnp.dot(a_ref[...], w_ref[:, c:e], preferred_element_type=f32)
 
+    return [lambda c=c: tile(c) for c in range(0, n, 256)]
+
 
 def source_rows(r_ref, cols):
     return [jnp.broadcast_to(r_ref[i : i + 1, cols], (8, lanes)) for i in range(6)]
@@ -84,6 +87,30 @@
 
 def added(total, term):
     return term if total is None else total + term
+
+
+def woven(main, side):
+    done = 0
+    for i, piece in enumerate(main):
+        while done < len(side) and done * len(main) <= i * len(side):
+            side[done]()
+            done += 1
+        piece()
+    for piece in side[done:]:
+        piece()
+
+
+def finish_pieces(j, acc_ref, own_ref, out_ref, more_ref):
+    points = out_ref.shape[2]
+
+    def turn():
+        turned = acc_ref[...].T
+        if more_ref is None:
+            out_ref[j] = turned[0:3, :points]
+        else:
+            out_ref[j] = turned[0:3, :points] + own_ref[0:3, :points] * turned[3:4, :points] + more_ref[j]
+
+    return [turn]
 
 
 def near_kernel(
@@ -104,12 +131,14 @@
     o1,
     a0,
     a1,
+    c0,
+    c1,
     feature_ref,
-    sums,
 ):
     cells = out_ref.shape[0]
     points = out_ref.shape[2]
     tiles = r0.shape[1] // lanes
+    blocks = 4
 
     def prepare(j, center, r_ref, w_ref):
         lane = lax.broadcasted_iota(jnp.int32, (8, lanes), 1)
@@ -126,46 +155,57 @@
         r_ref[...] = raw
         w_ref[...] = source_features(raw)
 
-    def evaluate(j, s_ref, r_ref, own_ref):
-        blocks = 4
-        for start in range(0, points, 8 * blocks):
-            acc = [[None] * blocks for _ in range(4)]
-            for c in range(tiles):
-                cols = slice(c * lanes, c * lanes + lanes)
-                src = source_rows(r_ref, cols)
-                for b in range(blocks):
-                    top = start + 8 * b
-                    h = lax.rsqrt(s_ref[top : top + 8, cols])
-                    cube = h * h * h
-                    whole = h + cube
-                    m = s_ref[points + top : points + top + 8, cols] * cube
-                    acc[3][b] = added(acc[3][b], m)
-                    for k in range(3):
-                        acc[k][b] = added(acc[k][b], whole * src[3 + k]) - m * src[k]
+    def chunk(start, s_ref, r_ref, acc_ref):
+        acc = [[None] * blocks for _ in range(4)]
+        for c in range(tiles):
+            cols = slice(c * lanes, c * lanes + lanes)
+            src = source_rows(r_ref, cols)
             for b in range(blocks):
                 top = start + 8 * b
-                for k in range(4):
-                    sums[top : top + 8, k : k + 1] = jnp.sum(acc[k][b], axis=1, keepdims=True)
-        flat = sums[...].T[0:4, :points]
-        out_ref[j] = flat[0:3] + own_ref[0:3, :points] * flat[3:4] + wall_ref[j]
-
-    def step(j, s_ref, r_ref, w_ref, own_ref, a_ref):
+                h = lax.rsqrt(s_ref[top : top + 8, cols])
+                cube = h * h * h
+                whole = h + cube
+                m = s_ref[points + top : points + top + 8, cols] * cube
+                acc[3][b] = added(acc[3][b], m)
+                for k in range(3):
+                    acc[k][b] = added(acc[k][b], whole * src[3 + k]) - m * src[k]
+        for b in range(blocks):
+            top = start + 8 * b
+            for k in range(4):
+                acc_ref[top : top + 8, k : k + 1] = jnp.sum(acc[k][b], axis=1, keepdims=True)
+
+    def step(j, r_ref, w_ref, own_ref, a_ref):
         center = prepare_own(j, point_ref, density_ref, weight_ref, feature_ref, own_ref, a_ref, 2)
         prepare(j, center, r_ref, w_ref)
-        products(a_ref, w_ref, s_ref)
-
+
+    def stage(j, now, later, last):
+        s_ref, r_ref, w_ref, own_ref, a_ref, acc_ref = now
+        next_s, next_r, next_w, next_own, next_a, next_acc = later
+        side = finish_pieces(jnp.maximum(j - 1, 0), next_acc, next_own, out_ref, wall_ref)
+        side += [lambda: step(last, next_r, next_w, next_own, next_a)]
+        side += product_tiles(next_a, next_w, next_s)
+        main = [lambda t=t: chunk(t, s_ref, r_ref, acc_ref) for t in range(0, points, 8 * blocks)]
+        woven(main, side)
+
+    even = (s0, r0, w0, o0, a0, c0)
+    odd = (s1, r1, w1, o1, a1, c1)
     start_features(feature_ref)
-    step(0, s0, r0, w0, o0, a0)
+    c0[...] = jnp.zeros_like(c0)
+    c1[...] = jnp.zeros_like(c1)
+    o1[...] = jnp.zeros_like(o1)
+    step(0, r0, w0, o0, a0)
+    for piece in product_tiles(a0, w0, s0):
+        piece()
 
     def body(i, carry):
         j = 2 * i
-        step(j + 1, s1, r1, w1, o1, a1)
-        evaluate(j, s0, r0, o0)
-        step(jnp.minimum(j + 2, cells - 1), s0, r0, w0, o0, a0)
-        evaluate(j + 1, s1, r1, o1)
+        stage(j, even, odd, j + 1)
+        stage(j + 1, odd, even, jnp.minimum(j + 2, cells - 1))
         return carry
 
     lax.fori_loop(0, cells // 2, body, 0)
+    for piece in finish_pieces(cells - 1, c1, o1, out_ref, wall_ref):
+        piece()
 
 
 def wall_kernel(
@@ -186,15 +226,18 @@
     o1,
     a0,
     a1,
+    c0,
+    c1,
     feature_ref,
-    sums,
-    columns,
+    p0,
+    p1,
+    pick_ref,
 ):
     cells = out_ref.shape[0]
     points = out_ref.shape[2]
     tiles = r0.shape[1] // lanes
+    blocks = 2
     lane = lax.broadcasted_iota(jnp.int32, (8, lanes), 1)
-    back_ref[...] = jnp.zeros_like(back_ref)
 
     def prepare(j, center, r_ref, w_ref):
         parts = []
@@ -207,40 +250,34 @@
         r_ref[...] = raw
         w_ref[...] = source_features(raw)
 
-    def evaluate(j, s_ref, r_ref, own_ref):
-        blocks = 2
-        columns[...] = own_ref[...].T
-        back = [[None] * 4 for _ in range(tiles)]
-        for start in range(0, points, 8 * blocks):
-            acc = [[None] * blocks for _ in range(4)]
-            own = [
-                [
-                    jnp.broadcast_to(columns[start + 8 * b : start + 8 * b + 8, k : k + 1], (8, lanes))
-                    for k in range(6)
-                ]
-                for b in range(blocks)
-            ]
-            for c in range(tiles):
-                cols = slice(c * lanes, c * lanes + lanes)
-                src = source_rows(r_ref, cols)
-                for b in range(blocks):
-                    top = start + 8 * b
-                    h = lax.rsqrt(s_ref[top : top + 8, cols])
-                    cube = h * h * h
-                    whole = h + cube
-                    m = s_ref[points + top : points + top + 8, cols] * cube
-                    n = s_ref[2 * points + top : 2 * points + top + 8, cols] * cube
-                    acc[3][b] = added(acc[3][b], m)
-                    back[c][3] = added(back[c][3], n)
-                    for k in range(3):
-                        acc[k][b] = added(acc[k][b], whole * src[3 + k]) - m * src[k]
-                        back[c][k] = added(back[c][k], whole * own[b][3 + k]) - n * own[b][k]
+    def chunk(start, s_ref, r_ref, acc_ref, own_ref, back):
+        acc = [[None] * blocks for _ in range(4)]
+        own = [
+            [own_ref[start + 8 * b : start + 8 * b + 8, k * lanes : k * lanes + lanes] for k in range(6)]
+            for b in range(blocks)
+        ]
+        for c in range(tiles):
+            cols = slice(c * lanes, c * lanes + lanes)
+            src = source_rows(r_ref, cols)
             for b in range(blocks):
                 top = start + 8 * b
-                for k in range(4):
-                    sums[top : top + 8, k : k + 1] = jnp.sum(acc[k][b], axis=1, keepdims=True)
-        flat = sums[...].T[0:4, :points]
-        out_ref[j] = flat[0:3] + own_ref[0:3, :points] * flat[3:4]
+                h = lax.rsqrt(s_ref[top : top + 8, cols])
+                cube = h * h * h
+                whole = h + cube
+                m = s_ref[points + top : points + top + 8, cols] * cube
+                n = s_ref[2 * points + top : 2 * points + top + 8, cols] * cube
+                acc[3][b] = added(acc[3][b], m)
+                back[c][3] = added(back[c][3], n)
+                for k in range(3):
+                    acc[k][b] = added(acc[k][b], whole * src[3 + k]) - m * src[k]
+                    back[c][k] = added(back[c][k], whole * own[b][3 + k]) - n * own[b][k]
+        for b in range(blocks):
+            top = start + 8 * b
+            for k in range(3):
+                line = acc[k][b] + own[b][k] * acc[3][b]
+                acc_ref[top : top + 8, k : k + 1] = jnp.sum(line, axis=1, keepdims=True)
+
+    def give_back(j, r_ref, back):
         for c in range(tiles):
             rows = [jnp.sum(back[c][k], axis=0, keepdims=True) for k in range(4)]
             rows = jnp.concatenate(rows + [jnp.zeros((4, lanes), f32)], axis=0)
@@ -252,44 +289,73 @@
                 kept = jnp.where((lane >= 64) == (odd == 1), moved, 0.0)
                 back_ref[patch // 2] += kept
 
-    def step(j, s_ref, r_ref, w_ref, own_ref, a_ref):
+    def step(j, r_ref, w_ref, own_ref, a_ref):
         center = prepare_own(j, point_ref, density_ref, weight_ref, feature_ref, own_ref, a_ref, 3)
         prepare(j, center, r_ref, w_ref)
-        products(a_ref, w_ref, s_ref)
-
+
+    def spread_pieces(a_ref, p_ref):
+        half = 3 * lanes
+
+        def positions():
+            p_ref[:, :half] = jnp.dot(a_ref[:points], pick_ref[:, :half], preferred_element_type=f32)
+
+        def loads():
+            p_ref[:, half:] = jnp.dot(a_ref[2 * points :], pick_ref[:, half:], preferred_element_type=f32)
+
+        return [positions, loads]
+
+    def stage(j, now, later, last):
+        s_ref, r_ref, w_ref, own_ref, a_ref, acc_ref, p_ref = now
+        next_s, next_r, next_w, next_own, next_a, next_acc, next_p = later
+        side = finish_pieces(jnp.maximum(j - 1, 0), next_acc, next_own, out_ref, None)
+        side += [lambda: step(last, next_r, next_w, next_own, next_a)]
+        side += product_tiles(next_a, next_w, next_s) + spread_pieces(next_a, next_p)
+        back = [[None] * 4 for _ in range(tiles)]
+        main = [lambda t=t: chunk(t, s_ref, r_ref, acc_ref, p_ref, back) for t in range(0, points, 8 * blocks)]
+        woven(main, side)
+        give_back(j, r_ref, back)
+
+    even = (s0, r0, w0, o0, a0, c0, p0)
+    odd = (s1, r1, w1, o1, a1, c1, p1)
+    back_ref[...] = jnp.zeros_like(back_ref)
     start_features(feature_ref)
-    own_ref_rows = jnp.zeros_like(o0)
-    o0[...] = own_ref_rows
-    o1[...] = own_ref_rows
-    step(0, s0, r0, w0, o0, a0)
+    feature = lax.broadcasted_iota(jnp.int32, pick_ref.shape, 0)
+    column = lax.broadcasted_iota(jnp.int32, pick_ref.shape, 1) // lanes
+    hit = (feature < 24) & (feature % 8 == column % 3)
+    pick_ref[...] = jnp.where(hit, jnp.where(column < 3, 1.0, -2.0), 0.0).astype(bf16)
+    c0[...] = jnp.zeros_like(c0)
+    c1[...] = jnp.zeros_like(c1)
+    o1[...] = jnp.zeros_like(o1)
+    step(0, r0, w0, o0, a0)
+    for piece in product_tiles(a0, w0, s0) + spread_pieces(a0, p0):
+        piece()
 
     def body(i, carry):
         j = 2 * i
-        step(j + 1, s1, r1, w1, o1, a1)
-        evaluate(j, s0, r0, o0)
-        step(jnp.minimum(j + 2, cells - 1), s0, r0, w0, o0, a0)
-        evaluate(j + 1, s1, r1, o1)
+        stage(j, even, odd, j + 1)
+        stage(j + 1, odd, even, jnp.minimum(j + 2, cells - 1))
         return carry
 
     lax.fori_loop(0, cells // 2, body, 0)
+    for piece in finish_pieces(cells - 1, c1, o1, out_ref, None):
+        piece()
 
 
 def scratch(points, kinds, tiles):
     wide = -(-points // lanes) * lanes
-    return [
-        pltpu.VMEM((kinds * points, tiles * lanes), f32),
+    pairs = [
         pltpu.VMEM((kinds * points, tiles * lanes), f32),
         pltpu.VMEM((8, tiles * lanes), f32),
-        pltpu.VMEM((8, tiles * lanes), f32),
-        pltpu.VMEM((depth, tiles * lanes), bf16),
         pltpu.VMEM((depth, tiles * lanes), bf16),
         pltpu.VMEM((8, wide), f32),
-        pltpu.VMEM((8, wide), f32),
         pltpu.VMEM((kinds * points, depth), bf16),
-        pltpu.VMEM((kinds * points, depth), bf16),
-        pltpu.VMEM((kinds * depth, wide), f32),
         pltpu.VMEM((wide, lanes), f32),
     ]
+    shapes = [shape for shape in pairs for _ in range(2)]
+    shapes += [pltpu.VMEM((kinds * depth, wide), f32)]
+    if kinds == 3:
+        shapes += [pltpu.VMEM((points, 6 * lanes), f32)] * 2 + [pltpu.VMEM((depth, 6 * lanes), bf16)]
+    return shapes
 
 
 def local(
@@ -310,7 +376,6 @@
     quarter = points // wall_count
     extra = quarter - lanes
     part = patch_pts // wall_count
-    wide = -(-points // lanes) * lanes
     vmem = pl.BlockSpec(memory_space=pltpu.VMEM)
     smem = pl.BlockSpec(memory_space=pltpu.SMEM)
     params = pltpu.CompilerParams(vmem_limit_bytes=60 * 2**20)
@@ -322,7 +387,9 @@
     ends = [mine[:, q, lanes:] for q in range(6)]
     tail = jnp.concatenate([ends[0], gap] + ends[:0:-1], axis=1)[:, None, :]
     block = jnp.concatenate([mine[:, :, :lanes], tail, jnp.zeros((cells, 1, lanes), f32)], axis=1)
-    gathered = lax.all_gather(block, "cell", axis=0, tiled=True)
+    groups = lax.axis_size("cell")
+    copies = jnp.broadcast_to(block[None], (groups,) + block.shape).reshape(groups * cells, 8, lanes)
+    gathered = lax.all_to_all(copies, "cell", split_axis=0, concat_axis=0, tiled=True)
 
     wall_raw = jnp.concatenate(
         [2.0 * wall_points, wall_density * wall_weights[:, None, :], jnp.zeros((patch_dev, 2, patch_pts), f32)],
@@ -341,9 +408,9 @@
         ),
         in_specs=[smem] + [vmem] * 4,
         out_specs=(vmem, vmem),
-        scratch_shapes=scratch(points, 3, tiles) + [pltpu.VMEM((wide, 8), f32)],
+        scratch_shapes=scratch(points, 3, tiles),
         compiler_params=params,
-        cost_estimate=pl.CostEstimate(flops=10**9, bytes_accessed=10**8, transcendentals=0),
+        cost_estimate=pl.CostEstimate(flops=7 * 10**10, bytes_accessed=10**7, transcendentals=0),
         name="wall_pairs",
     )(near_wall, patches, cell_points, cell_density, cell_weights)
 
@@ -356,17 +423,22 @@
         out_specs=vmem,
         scratch_shapes=scratch(points, 2, tiles),
         compiler_params=params,
-        cost_estimate=pl.CostEstimate(flops=10**9, bytes_accessed=10**8, transcendentals=0),
+        cost_estimate=pl.CostEstimate(flops=7 * 10**10, bytes_accessed=10**7, transcendentals=0),
         name="near_pairs",
     )(near_ids, gathered, cell_points, cell_density, cell_weights, wall_term)
 
+    pairs = patch_dev // 2
     total = total.reshape(cells, 3, wall_count, quarter).transpose(2, 0, 1, 3)
-    share = jnp.sum(lax.all_to_all(total, "wall", split_axis=0, concat_axis=0, tiled=True), axis=0)
+    back = back[:, :3, :].reshape(wall_count, pairs, 3, lanes)
+    both = jnp.concatenate(
+        [total.reshape(wall_count, -1, lanes), back.reshape(wall_count, -1, lanes)], axis=1
+    )
+    both = lax.all_to_all(both, "wall", split_axis=0, concat_axis=0, tiled=True)
+    cut = cells * 3 * quarter // lanes
+    share = jnp.sum(both[:, :cut], axis=0).reshape(cells, 3, quarter)
     own = lax.dynamic_slice_in_dim(cell_density, wall_index * quarter, quarter, 2)
     velocity = 0.5 * own + two_stokes_factor * share
-
-    back = lax.all_to_all(back[:, :3, :], "wall", split_axis=0, concat_axis=0, tiled=True)
-    back = back.reshape(wall_count, patch_dev // 2, 3, 2, part).transpose(1, 3, 2, 0, 4)
+    back = both[:, cut:].reshape(wall_count, pairs, 3, 2, part).transpose(1, 3, 2, 0, 4)
     wall_velocity = 0.5 * wall_density + two_stokes_factor * back.reshape(patch_dev, 3, patch_pts)
     return (velocity, wall_velocity)
 

time: 206 us -> 182 us (0.88); the launches traced: 202 us -> 182 us
  between operations: 14.2 us -> 0.89 us
  waiting for transfers between devices: 15.8 us -> 4.45 us
  blocking collectives: 0 us -> 10.3 us
  Pallas kernels: 144 us -> 134 us
  starting transfers between devices: 11.9 us -> 15.2 us
    all_to_all x0 -> x1, blocking collectives: none -> 10.3 us  [local(): both = lax.all_to_all(both, 'wall', split_axis=0, concat_axis=0, tiled=True)]
    all_to_all x2 -> x1, waiting for transfers between devices: 10.2 us -> 0.01 us  [local(): lax.all_to_all(copies, 'cell', split_axis=0, concat_axis=0, tiled=True)]
    pallas_call x1, Pallas kernels: 72.9 us -> 64.4 us  [local(): pl.pallas_call(wall_kernel, out_shape=(jax.ShapeDtypeStruct((cells, 3, po...]
    all_to_all x2 -> x1, starting transfers between devices: 7.04 us -> 10.3 us  [local(): lax.all_to_all(copies, 'cell', split_axis=0, concat_axis=0, tiled=True)]
    broadcast_in_dim x0 -> x1, local copies, waits for them, and re-layouts: none -> 2.45 us  [local(): jnp.broadcast_to(block[None], (groups,) + block.shape)]
  transfers between devices with their start and end apart: 4 -> 2, of which waited for: 3 -> 1; matrix products, arithmetic and copies ran while one was open for 5% -> 3% of each run, Pallas kernels for 36% -> 35%
where the time goes in v2:
time: 182 us
  Pallas kernels  134 us (74%)
  starting transfers between devices  15.2 us (8%)
  local copies, waits for them, and re-layouts  12.6 us (7%)
  blocking collectives  10.3 us (6%)
  waiting for transfers between devices  4.45 us (2%)
  other arithmetic  4.06 us (2%)
    pallas_call x1, Pallas kernels, local(): pl.pallas_call(near_kernel, out_shape=jax.ShapeDtypeStruct((cells, 3, poi...  69.9 us
    pallas_call x1, Pallas kernels, local(): pl.pallas_call(wall_kernel, out_shape=(jax.ShapeDtypeStruct((cells, 3, po...  64.4 us
    all_to_all x1, starting transfers between devices, local(): lax.all_to_all(copies, 'cell', split_axis=0, concat_axis=0, tiled=True)  10.3 us
    all_to_all x1, blocking collectives, local(): both = lax.all_to_all(both, 'wall', split_axis=0, concat_axis=0, tiled=True)  10.3 us
    all_to_all x1, starting transfers between devices, local(): lax.all_to_all(wall_raw, 'wall', split_axis=0, concat_axis=0, tiled=True)  4.84 us
    all_to_all x1, waiting for transfers between devices, local(): lax.all_to_all(wall_raw, 'wall', split_axis=0, concat_axis=0, tiled=True)  4.44 us
  transfers between devices with their start and end apart: 2, of which 1 were waited for; matrix products, arithmetic and copies ran while one was open for 3% of the time, Pallas kernels for 35%

profile of v2, /device:TPU:1, one launch (start us, length us, event | category | flops | bytes accessed | tf_op | source)
XLA Modules:
  0.0 181.7 jit_solution(9852674974346325820)
XLA Ops:
  0.7 1.2 broadcast_multiply_fusion.2
  2.1 0.5 reshape.32
  2.6 0.5 copy.63
  3.1 1.4 reshape.33
  4.5 4.8 %all-to-all-start.1 = ((f32[128,8,128]{2,1,0:T(8,128)}), f32[128,8,128]{2,1,0:T(8,128)S(1)}, u32[]{:S(2)}, u32[]{:S(2)}) async-start(f32[128,8,128]{2,1,0:T(8,128)} %reshape.33), calls=%async_computation.1 | async-start | bytes 1048576 | tf_op jit(solution)/shard_map/all_to_all | solution.py:400
  9.6 0.9 copy.47.density_ref
  10.5 0.9 copy.56.point_ref
  11.8 0.7 copy.53.ids_ref
  12.6 0.6 multiply_add_fusion.2.ids_ref
  13.2 4.4 %all-to-all-done.1.patch_ref = f32[128,8,128]{2,1,0:T(8,128)S(1)} async-done(((f32[128,8,128]{2,1,0:T(8,128)}), f32[128,8,128]{2,1,0:T(8,128)S(1)}, u32[]{:S(2)}, u32[]{:S(2)}) %all-to-all-start.1) | async-done | bytes 524320 | tf_op jit(solution)/shard_map/all_to_all | solution.py:400
  17.7 2.4 %broadcast_in_dim.23 = f32[32,32,8,128]{3,2,1,0:T(8,128)} broadcast(f32[32,8,128]{2,1,0:T(8,128)S(1)} %copy.51), dimensions={1,2,3} | broadcast | bytes 4325376 | tf_op jit(solution)/shard_map/broadcast_in_dim | solution.py:391
  20.1 10.3 %all-to-all-start = ((f32[1024,8,128]{2,1,0:T(8,128)}), f32[1024,8,128]{2,1,0:T(8,128)}, u32[]{:S(2)}, u32[]{:S(2)}) async-start(f32[1024,8,128]{2,1,0:T(8,128)} %bitcast.26), calls=%async_computation | async-start | bytes 8388608 | tf_op jit(solution)/shard_map/all_to_all | solution.py:392
  30.4 64.4 %wall_pairs.1 = (f32[32,3,544]{2,1,0:T(4,128)}, f32[128,8,128]{2,1,0:T(8,128)}) custom-call(s32[32,8]{1,0:T(8,128)} %copy.53.ids_ref, f32[128,8,128]{2,1,0:T(8,128)} %copy-done.3, f32[32,3,544]{2,1,0:T(4,128)} %copy.56.point_ref, f32[32,3,544]{2,1,0:T(4,128)} %copy.47.density_ref, f32[32,544]{1,0:T(8,128)} %weight_ref.3), custom_call_target="tpu_custom_call" | custom-call | flops 70000001024 | bytes 10000000 | tf_op jit(solution)/shard_map/wall_pairs/pallas_call | solution.py:403
  94.8 1.1 slice.37
  96.0 69.9 %near_pairs.1 = f32[32,3,544]{2,1,0:T(4,128)} custom-call(s32[32,8]{1,0:T(8,128)} %multiply_add_fusion.2.ids_ref, f32[1024,8,128]{2,1,0:T(8,128)} %all-to-all-done.gathered_ref, f32[32,3,544]{2,1,0:T(4,128)} %copy.56.point_ref, f32[32,3,544]{2,1,0:T(4,128)} %copy.47.density_ref, f32[32,544]{1,0:T(8,128)} %weight_ref.3, f32[32,3,544]{2,1,0:T(4,128)} %get-tuple-element.4.wall_ref), custom_call_target="tpu_custom_call" | custom-call | flops 70000001024 | bytes 10000000 | tf_op jit(solution)/shard_map/near_pairs/pallas_call | solution.py:419
  165.9 1.0 copy.58
  166.9 0.3 reshape.34
  167.2 0.3 copy.59
  167.5 0.4 reshape.35
  168.0 10.3 %all_to_all.15 = f32[4,198,128]{2,1,0:T(8,128)S(1)} all-to-all(f32[4,198,128]{2,1,0:T(8,128)S(1)} %pad_maximum_fusion), channel_id=1, replica_groups=mesh['cell'=32,'wall'=4] {'wall'}, dimensions={0} | all-to-all | bytes 811008 | tf_op jit(solution)/shard_map/all_to_all | solution.py:436
  178.8 0.3 mul.96
  179.1 0.7 multiply_add_fusion
  179.9 1.1 multiply_add_fusion.1
  181.0 0.7 copy.61
  (39 shorter events, 1.7 us)
Async XLA Ops:
  0.6 8.8 %copy-start = (f32[32,3,544]{2,0,1:T(8,128)S(1)}, f32[32,3,544]{2,0,1:T(8,128)}, u32[]{:S(2)}) copy-start(f32[32,3,544]{2,0,1:T(8,128)} %param.10) | copy-start | bytes 626692
  0.6 8.7 %copy-start.4 = (f32[32,544]{1,0:T(8,128)S(1)}, f32[32,544]{1,0:T(8,128)}, u32[]{:S(2)}) copy-start(f32[32,544]{1,0:T(8,128)} %weight_ref.3) | copy-start | bytes 208900
  0.7 8.7 %copy-start.1 = (f32[32,3,544]{2,0,1:T(8,128)S(1)}, f32[32,3,544]{2,0,1:T(8,128)}, u32[]{:S(2)}) copy-start(f32[32,3,544]{2,0,1:T(8,128)} %param.9) | copy-start | bytes 626692
  2.6 9.2 %copy-start.5 = (s32[32,8]{0,1:T(8,128)S(1)}, s32[32,8]{0,1:T(8,128)}, u32[]{:S(2)}) copy-start(s32[32,8]{0,1:T(8,128)} %param.14) | copy-start | bytes 3076
  2.6 9.9 %copy-start.6 = (s32[32,8]{0,1:T(8,128)S(1)}, s32[32,8]{0,1:T(8,128)}, u32[]{:S(2)}) copy-start(s32[32,8]{0,1:T(8,128)} %param.12) | copy-start | bytes 3076
  2.6 9.9 %copy-start.7 = (s32[32,8]{0,1:T(8,128)S(1)}, s32[32,8]{0,1:T(8,128)}, u32[]{:S(2)}) copy-start(s32[32,8]{0,1:T(8,128)} %param.13) | copy-start | bytes 3076
  4.5 13.1 %all-to-all-start.1 = ((f32[128,8,128]{2,1,0:T(8,128)}), f32[128,8,128]{2,1,0:T(8,128)S(1)}, u32[]{:S(2)}, u32[]{:S(2)}) async-start(f32[128,8,128]{2,1,0:T(8,128)} %reshape.33), calls=%async_computation.1 | async-start | bytes 1048576 | tf_op jit(solution)/shard_map/all_to_all | solution.py:400
  17.7 2.5 %copy-start.3 = (f32[128,8,128]{2,1,0:T(8,128)}, f32[128,8,128]{2,1,0:T(8,128)S(1)}, u32[]{:S(2)}) copy-start(f32[128,8,128]{2,1,0:T(8,128)S(1)} %all-to-all-done.1.patch_ref) | copy-start | bytes 1572868
  20.1 75.9 %all-to-all-start = ((f32[1024,8,128]{2,1,0:T(8,128)}), f32[1024,8,128]{2,1,0:T(8,128)}, u32[]{:S(2)}, u32[]{:S(2)}) async-start(f32[1024,8,128]{2,1,0:T(8,128)} %bitcast.26), calls=%async_computation | async-start | bytes 8388608 | tf_op jit(solution)/shard_map/all_to_all | solution.py:392
  165.9 13.2 %copy-start.2 = (f32[64,3,256]{2,0,1:T(8,128)S(1)}, f32[64,3,256]{2,0,1:T(8,128)}, u32[]{:S(2)}) copy-start(f32[64,3,256]{2,0,1:T(8,128)} %param.16) | copy-start | bytes 589828

commit v3 on v2

--- a/solution.py
+++ b/solution.py
@@ -341,6 +341,58 @@
         piece()
 
 
+def exchange_kernel(count, x_ref, out_ref, sent, received, kept):
+    me = lax.axis_index("wall")
+    barrier = pltpu.get_barrier_semaphore()
+    for d in range(1, count):
+        peer = lax.rem(me + d, count)
+        pl.semaphore_signal(barrier, inc=1, device_id={"wall": peer}, device_id_type=pl.DeviceIdType.MESH)
+    own = pltpu.make_async_copy(x_ref.at[me], out_ref.at[me], kept)
+    own.start()
+    pl.semaphore_wait(barrier, count - 1)
+    copies = []
+    for d in range(1, count):
+        peer = lax.rem(me + d, count)
+        copy = pltpu.make_async_remote_copy(
+            src_ref=x_ref.at[peer],
+            dst_ref=out_ref.at[me],
+            send_sem=sent.at[d - 1],
+            recv_sem=received.at[d - 1],
+            device_id={"wall": peer},
+            device_id_type=pl.DeviceIdType.MESH,
+        )
+        copy.start()
+        copies.append(copy)
+    own.wait()
+    for copy in copies:
+        copy.wait()
+
+
+def exchange(x, number):
+    count = x.shape[0]
+
+    def kernel(*refs):
+        exchange_kernel(count, *refs)
+
+    vmem = pl.BlockSpec(memory_space=pltpu.VMEM)
+    return pl.pallas_call(
+        kernel,
+        out_shape=jax.ShapeDtypeStruct(x.shape, f32),
+        in_specs=[vmem],
+        out_specs=vmem,
+        scratch_shapes=[
+            pltpu.SemaphoreType.DMA((count - 1,)),
+            pltpu.SemaphoreType.DMA((count - 1,)),
+            pltpu.SemaphoreType.DMA,
+        ],
+        compiler_params=pltpu.CompilerParams(
+            collective_id=number, has_side_effects=True, vmem_limit_bytes=16 * 2**20
+        ),
+        cost_estimate=pl.CostEstimate(flops=5 * 10**9, bytes_accessed=10**6, transcendentals=0),
+        name="exchange_%d" % number,
+    )(x)
+
+
 def scratch(points, kinds, tiles):
     wide = -(-points // lanes) * lanes
     pairs = [
@@ -396,8 +448,8 @@
         axis=1,
     )
     wall_raw = wall_raw.reshape(patch_dev // 2, 2, 8, wall_count, part).transpose(3, 0, 2, 1, 4)
-    wall_raw = wall_raw.reshape(wall_count * (patch_dev // 2), 8, 2 * part)
-    patches = lax.all_to_all(wall_raw, "wall", split_axis=0, concat_axis=0, tiled=True)
+    wall_raw = wall_raw.reshape(wall_count, (patch_dev // 2) * 8, 2 * part)
+    patches = exchange(wall_raw, 0).reshape(wall_count * (patch_dev // 2), 8, 2 * part)
 
     tiles = near_wall.shape[1] * part // lanes
     wall_term, back = pl.pallas_call(
@@ -433,7 +485,7 @@
     both = jnp.concatenate(
         [total.reshape(wall_count, -1, lanes), back.reshape(wall_count, -1, lanes)], axis=1
     )
-    both = lax.all_to_all(both, "wall", split_axis=0, concat_axis=0, tiled=True)
+    both = exchange(both, 1)
     cut = cells * 3 * quarter // lanes
     share = jnp.sum(both[:, :cut], axis=0).reshape(cells, 3, quarter)
     own = lax.dynamic_slice_in_dim(cell_density, wall_index * quarter, quarter, 2)

time: 182 us -> 180 us (0.989)
  Pallas kernels: 134 us -> 153 us
  blocking collectives: 10.3 us -> 0 us
  starting transfers between devices: 15.2 us -> 9.8 us
  waiting for transfers between devices: 4.45 us -> 0.01 us
    pallas_call x0 -> x2, Pallas kernels: none -> 18.4 us  [exchange(): pl.pallas_call(kernel, out_shape=jax.ShapeDtypeStruct(x.shape, f32), in_s...]
    all_to_all x1 -> x0, blocking collectives: 10.3 us -> none  [local(): both = lax.all_to_all(both, 'wall', split_axis=0, concat_axis=0, tiled=True)]
    all_to_all x1 -> x0, starting transfers between devices: 4.84 us -> none  [local(): lax.all_to_all(wall_raw, 'wall', split_axis=0, concat_axis=0, tiled=True)]
    all_to_all x1 -> x0, waiting for transfers between devices: 4.44 us -> none  [local(): lax.all_to_all(wall_raw, 'wall', split_axis=0, concat_axis=0, tiled=True)]
    unnamed x22 -> x26, local copies, waits for them, and re-layouts: 3.32 us -> 4.15 us
  transfers between devices with their start and end apart: 2 -> 1, of which waited for: 1 -> 0; matrix products, arithmetic and copies ran while one was open for 3% -> 3% of each run, Pallas kernels for 35% -> 41%
where the time goes in v3:
time: 180 us
  Pallas kernels  153 us (85%)
  local copies, waits for them, and re-layouts  12.6 us (7%)
  starting transfers between devices  9.8 us (5%)
  other arithmetic  3.95 us (2%)
    pallas_call x1, Pallas kernels, local(): pl.pallas_call(near_kernel, out_shape=jax.ShapeDtypeStruct((cells, 3, poi...  70.1 us
    pallas_call x1, Pallas kernels, local(): pl.pallas_call(wall_kernel, out_shape=(jax.ShapeDtypeStruct((cells, 3, po...  64.3 us
    pallas_call x2, Pallas kernels, exchange(): pl.pallas_call(kernel, out_shape=jax.ShapeDtypeStruct(x.shape, f32), in_s...  18.4 us
    all_to_all x1, starting transfers between devices, local(): lax.all_to_all(copies, 'cell', split_axis=0, concat_axis=0, tiled=True)  9.8 us
    unnamed x26, local copies, waits for them, and re-layouts  4.15 us
  transfers between devices with their start and end apart: 1, of which 0 were waited for; matrix products, arithmetic and copies ran while one was open for 3% of the time, Pallas kernels for 41%

profile of v3, /device:TPU:1, one launch (start us, length us, event | category | flops | bytes accessed | tf_op | source)
XLA Modules:
  0.0 180.0 jit_solution(18437925751847525338)
XLA Ops:
  0.6 1.1 broadcast_multiply_fusion
  2.3 2.4 %broadcast_in_dim.23 = f32[32,32,8,128]{3,2,1,0:T(8,128)} broadcast(f32[32,8,128]{2,1,0:T(8,128)S(1)} %copy.40), dimensions={1,2,3} | broadcast | bytes 4325376 | tf_op jit(solution)/shard_map/broadcast_in_dim | solution.py:443
  4.8 9.8 %all-to-all-start = ((f32[1024,8,128]{2,1,0:T(8,128)}), f32[1024,8,128]{2,1,0:T(8,128)}, u32[]{:S(2)}, u32[]{:S(2)}) async-start(f32[1024,8,128]{2,1,0:T(8,128)} %bitcast.28), calls=%async_computation | async-start | bytes 8388608 | tf_op jit(solution)/shard_map/all_to_all | solution.py:444
  14.6 0.9 copy.36.density_ref
  15.5 0.9 copy.45.point_ref
  16.6 0.5 reshape.35
  17.1 0.5 copy.52
  17.6 0.6 reshape.36.refs_0_
  18.2 10.1 %exchange_0.1 = f32[4,256,128]{2,1,0:T(8,128)S(1)} custom-call(f32[4,256,128]{2,1,0:T(8,128)S(1)} %reshape.36.refs_0_), custom_call_target="tpu_custom_call" | custom-call | flops 5000000000 | bytes 1000000 | tf_op jit(solution)/shard_map/exchange_0/pallas_call | solution.py:378
  28.3 0.8 copy-done
  29.1 0.7 copy.42.ids_ref
  30.0 64.3 %wall_pairs.1 = (f32[32,3,544]{2,1,0:T(4,128)}, f32[128,8,128]{2,1,0:T(8,128)}) custom-call(s32[32,8]{1,0:T(8,128)} %copy.42.ids_ref, f32[128,8,128]{2,1,0:T(8,128)} %bitcast.27, f32[32,3,544]{2,1,0:T(4,128)} %copy.45.point_ref, f32[32,3,544]{2,1,0:T(4,128)} %copy.36.density_ref, f32[32,544]{1,0:T(8,128)} %weight_ref.3), custom_call_target="tpu_custom_call" | custom-call | flops 70000001024 | bytes 10000000 | tf_op jit(solution)/shard_map/wall_pairs/pallas_call | solution.py:455
  94.3 1.1 slice.37
  95.5 0.6 multiply_add_fusion.2.ids_ref
  96.1 70.1 %near_pairs.1 = f32[32,3,544]{2,1,0:T(4,128)} custom-call(s32[32,8]{1,0:T(8,128)} %multiply_add_fusion.2.ids_ref, f32[1024,8,128]{2,1,0:T(8,128)} %all-to-all-done.gathered_ref, f32[32,3,544]{2,1,0:T(4,128)} %copy.45.point_ref, f32[32,3,544]{2,1,0:T(4,128)} %copy.36.density_ref, f32[32,544]{1,0:T(8,128)} %weight_ref.3, f32[32,3,544]{2,1,0:T(4,128)} %get-tuple-element.4.wall_ref), custom_call_target="tpu_custom_call" | custom-call | flops 70000001024 | bytes 10000000 | tf_op jit(solution)/shard_map/near_pairs/pallas_call | solution.py:471
  166.2 1.0 copy.47
  167.2 0.3 reshape.38
  167.5 0.3 copy.48
  167.8 0.4 reshape.39
  168.2 8.3 %exchange_1.1 = f32[4,198,128]{2,1,0:T(8,128)S(1)} custom-call(f32[4,198,128]{2,1,0:T(8,128)S(1)} %pad_maximum_fusion.refs_0_), custom_call_target="tpu_custom_call" | custom-call | flops 5000000000 | bytes 1000000 | tf_op jit(solution)/shard_map/exchange_1/pallas_call | solution.py:378
  177.2 0.3 mul.96
  177.4 0.7 multiply_add_fusion
  178.3 1.1 multiply_add_fusion.1
  179.4 0.7 copy.50
  (42 shorter events, 1.7 us)
Async XLA Ops:
  4.7 9.8 %copy-start.1 = (f32[32,3,544]{2,0,1:T(8,128)S(1)}, f32[32,3,544]{2,0,1:T(8,128)}, u32[]{:S(2)}) copy-start(f32[32,3,544]{2,0,1:T(8,128)} %param.10) | copy-start | bytes 626692
  4.8 10.7 %copy-start.2 = (f32[32,3,544]{2,0,1:T(8,128)S(1)}, f32[32,3,544]{2,0,1:T(8,128)}, u32[]{:S(2)}) copy-start(f32[32,3,544]{2,0,1:T(8,128)} %param.9) | copy-start | bytes 626692
  4.8 11.7 %copy-start.3 = (f32[64,3,256]{2,0,1:T(8,128)S(1)}, f32[64,3,256]{2,0,1:T(8,128)}, u32[]{:S(2)}) copy-start(f32[64,3,256]{2,0,1:T(8,128)} %param.16) | copy-start | bytes 589828
  4.8 11.7 %copy-start.5 = (f32[64,3,256]{2,0,1:T(8,128)S(1)}, f32[64,3,256]{2,0,1:T(8,128)}, u32[]{:S(2)}) copy-start(f32[64,3,256]{2,0,1:T(8,128)} %param.15) | copy-start | bytes 589828
  4.8 11.7 %copy-start.6 = (f32[64,256]{1,0:T(8,128)S(1)}, f32[64,256]{1,0:T(8,128)}, u32[]{:S(2)}) copy-start(f32[64,256]{1,0:T(8,128)} %param.17) | copy-start | bytes 196612
  4.8 91.3 %all-to-all-start = ((f32[1024,8,128]{2,1,0:T(8,128)}), f32[1024,8,128]{2,1,0:T(8,128)}, u32[]{:S(2)}, u32[]{:S(2)}) async-start(f32[1024,8,128]{2,1,0:T(8,128)} %bitcast.28), calls=%async_computation | async-start | bytes 8388608 | tf_op jit(solution)/shard_map/all_to_all | solution.py:444
  18.2 10.9 %copy-start.7 = (s32[32,8]{0,1:T(8,128)S(1)}, s32[32,8]{0,1:T(8,128)}, u32[]{:S(2)}) copy-start(s32[32,8]{0,1:T(8,128)} %param.14) | copy-start | bytes 3076
  18.2 11.6 %copy-start.8 = (s32[32,8]{0,1:T(8,128)S(1)}, s32[32,8]{0,1:T(8,128)}, u32[]{:S(2)}) copy-start(s32[32,8]{0,1:T(8,128)} %param.12) | copy-start | bytes 3076
  18.2 11.7 %copy-start.9 = (s32[32,8]{0,1:T(8,128)S(1)}, s32[32,8]{0,1:T(8,128)}, u32[]{:S(2)}) copy-start(s32[32,8]{0,1:T(8,128)} %param.13) | copy-start | bytes 3076
  28.3 0.8 copy-start
  168.2 9.2 %copy-start.4 = (f32[64,3,256]{2,0,1:T(8,128)S(1)}, f32[64,3,256]{2,0,1:T(8,128)}, u32[]{:S(2)}) copy-start(f32[64,3,256]{2,0,1:T(8,128)} %param.16) | copy-start | bytes 589828

commit v4 on v3

--- a/solution.py
+++ b/solution.py
@@ -152,7 +152,7 @@
             tail = jnp.where((lane >= 8 * k) & (lane < 8 * k + 8), last, tail)
         parts.append(jnp.where(lane < 64, tail - center, 0.0))
         raw = jnp.concatenate(parts, axis=1)
-        r_ref[...] = raw
+        r_ref[...] = jnp.concatenate([-raw[0:3], raw[3:8]], axis=0)
         w_ref[...] = source_features(raw)
 
     def chunk(start, s_ref, r_ref, acc_ref):
@@ -168,7 +168,7 @@
                 m = s_ref[points + top : points + top + 8, cols] * cube
                 acc[3][b] = added(acc[3][b], m)
                 for k in range(3):
-                    acc[k][b] = added(acc[k][b], whole * src[3 + k]) - m * src[k]
+                    acc[k][b] = added(acc[k][b], whole * src[3 + k]) + m * src[k]
         for b in range(blocks):
             top = start + 8 * b
             for k in range(4):
@@ -247,7 +247,7 @@
             two = pltpu.roll(patch_ref[right // 2], 64 * (1 - right % 2), 1)
             parts.append(jnp.where(lane < 64, one, two) - center)
         raw = jnp.concatenate(parts, axis=1)
-        r_ref[...] = raw
+        r_ref[...] = jnp.concatenate([-raw[0:3], raw[3:8]], axis=0)
         w_ref[...] = source_features(raw)
 
     def chunk(start, s_ref, r_ref, acc_ref, own_ref, back):
@@ -269,19 +269,19 @@
                 acc[3][b] = added(acc[3][b], m)
                 back[c][3] = added(back[c][3], n)
                 for k in range(3):
-                    acc[k][b] = added(acc[k][b], whole * src[3 + k]) - m * src[k]
-                    back[c][k] = added(back[c][k], whole * own[b][3 + k]) - n * own[b][k]
+                    acc[k][b] = added(acc[k][b], whole * src[3 + k]) + m * src[k]
+                    back[c][k] = added(back[c][k], whole * own[b][3 + k]) + n * own[b][k]
         for b in range(blocks):
             top = start + 8 * b
             for k in range(3):
-                line = acc[k][b] + own[b][k] * acc[3][b]
+                line = acc[k][b] - own[b][k] * acc[3][b]
                 acc_ref[top : top + 8, k : k + 1] = jnp.sum(line, axis=1, keepdims=True)
 
     def give_back(j, r_ref, back):
         for c in range(tiles):
             rows = [jnp.sum(back[c][k], axis=0, keepdims=True) for k in range(4)]
             rows = jnp.concatenate(rows + [jnp.zeros((4, lanes), f32)], axis=0)
-            term = rows + r_ref[:, c * lanes : c * lanes + lanes] * rows[3:4, :]
+            term = rows - r_ref[:, c * lanes : c * lanes + lanes] * rows[3:4, :]
             for half in range(2):
                 patch = ids_ref[j, 2 * c + half]
                 odd = patch % 2
@@ -322,7 +322,7 @@
     feature = lax.broadcasted_iota(jnp.int32, pick_ref.shape, 0)
     column = lax.broadcasted_iota(jnp.int32, pick_ref.shape, 1) // lanes
     hit = (feature < 24) & (feature % 8 == column % 3)
-    pick_ref[...] = jnp.where(hit, jnp.where(column < 3, 1.0, -2.0), 0.0).astype(bf16)
+    pick_ref[...] = jnp.where(hit, jnp.where(column < 3, -1.0, -2.0), 0.0).astype(bf16)
     c0[...] = jnp.zeros_like(c0)
     c1[...] = jnp.zeros_like(c1)
     o1[...] = jnp.zeros_like(o1)

time: 180 us -> 179 us (level)
  Pallas kernels: 153 us -> 151 us
where the time goes in v4:
time: 179 us; the launch traced here: 178 us
  Pallas kernels  151 us (84%)
  local copies, waits for them, and re-layouts  12.6 us (7%)
  starting transfers between devices  9.8 us (5%)
  other arithmetic  3.95 us (2%)
    pallas_call x1, Pallas kernels, local(): pl.pallas_call(near_kernel, out_shape=jax.ShapeDtypeStruct((cells, 3, poi...  69 us
    pallas_call x1, Pallas kernels, local(): pl.pallas_call(wall_kernel, out_shape=(jax.ShapeDtypeStruct((cells, 3, po...  63.7 us
    pallas_call x2, Pallas kernels, exchange(): pl.pallas_call(kernel, out_shape=jax.ShapeDtypeStruct(x.shape, f32), in_s...  18.5 us
    all_to_all x1, starting transfers between devices, local(): lax.all_to_all(copies, 'cell', split_axis=0, concat_axis=0, tiled=True)  9.8 us
    unnamed x26, local copies, waits for them, and re-layouts  4.15 us
  transfers between devices with their start and end apart: 1, of which 0 were waited for; matrix products, arithmetic and copies ran while one was open for 3% of the time, Pallas kernels for 41%

profile of v4, /device:TPU:1, one launch (start us, length us, event | category | flops | bytes accessed | tf_op | source)
XLA Modules:
  0.0 178.4 jit_solution(15306503174407775502)
XLA Ops:
  0.6 1.1 broadcast_multiply_fusion
  2.3 2.4 %broadcast_in_dim.23 = f32[32,32,8,128]{3,2,1,0:T(8,128)} broadcast(f32[32,8,128]{2,1,0:T(8,128)S(1)} %copy.40), dimensions={1,2,3} | broadcast | bytes 4325376 | tf_op jit(solution)/shard_map/broadcast_in_dim | solution.py:443
  4.8 9.8 %all-to-all-start = ((f32[1024,8,128]{2,1,0:T(8,128)}), f32[1024,8,128]{2,1,0:T(8,128)}, u32[]{:S(2)}, u32[]{:S(2)}) async-start(f32[1024,8,128]{2,1,0:T(8,128)} %bitcast.28), calls=%async_computation | async-start | bytes 8388608 | tf_op jit(solution)/shard_map/all_to_all | solution.py:444
  14.6 0.9 copy.36.density_ref
  15.5 0.9 copy.45.point_ref
  16.6 0.5 reshape.35
  17.1 0.5 copy.52
  17.6 0.6 reshape.36.refs_0_
  18.2 10.1 %exchange_0.1 = f32[4,256,128]{2,1,0:T(8,128)S(1)} custom-call(f32[4,256,128]{2,1,0:T(8,128)S(1)} %reshape.36.refs_0_), custom_call_target="tpu_custom_call" | custom-call | flops 5000000000 | bytes 1000000 | tf_op jit(solution)/shard_map/exchange_0/pallas_call | solution.py:378
  28.3 0.8 copy-done
  29.1 0.7 copy.42.ids_ref
  30.0 63.7 %wall_pairs.1 = (f32[32,3,544]{2,1,0:T(4,128)}, f32[128,8,128]{2,1,0:T(8,128)}) custom-call(s32[32,8]{1,0:T(8,128)} %copy.42.ids_ref, f32[128,8,128]{2,1,0:T(8,128)} %bitcast.27, f32[32,3,544]{2,1,0:T(4,128)} %copy.45.point_ref, f32[32,3,544]{2,1,0:T(4,128)} %copy.36.density_ref, f32[32,544]{1,0:T(8,128)} %weight_ref.3), custom_call_target="tpu_custom_call" | custom-call | flops 70000001024 | bytes 10000000 | tf_op jit(solution)/shard_map/wall_pairs/pallas_call | solution.py:455
  93.6 1.1 slice.37
  94.8 0.6 multiply_add_fusion.2.ids_ref
  95.4 69.0 %near_pairs.1 = f32[32,3,544]{2,1,0:T(4,128)} custom-call(s32[32,8]{1,0:T(8,128)} %multiply_add_fusion.2.ids_ref, f32[1024,8,128]{2,1,0:T(8,128)} %all-to-all-done.gathered_ref, f32[32,3,544]{2,1,0:T(4,128)} %copy.45.point_ref, f32[32,3,544]{2,1,0:T(4,128)} %copy.36.density_ref, f32[32,544]{1,0:T(8,128)} %weight_ref.3, f32[32,3,544]{2,1,0:T(4,128)} %get-tuple-element.4.wall_ref), custom_call_target="tpu_custom_call" | custom-call | flops 70000001024 | bytes 10000000 | tf_op jit(solution)/shard_map/near_pairs/pallas_call | solution.py:471
  164.5 1.0 copy.47
  165.5 0.3 reshape.38
  165.8 0.3 copy.48
  166.1 0.4 reshape.39
  166.6 8.4 %exchange_1.1 = f32[4,198,128]{2,1,0:T(8,128)S(1)} custom-call(f32[4,198,128]{2,1,0:T(8,128)S(1)} %pad_maximum_fusion.refs_0_), custom_call_target="tpu_custom_call" | custom-call | flops 5000000000 | bytes 1000000 | tf_op jit(solution)/shard_map/exchange_1/pallas_call | solution.py:378
  175.5 0.3 mul.96
  175.8 0.7 multiply_add_fusion
  176.7 1.1 multiply_add_fusion.1
  177.7 0.7 copy.50
  (42 shorter events, 1.7 us)
Async XLA Ops:
  4.7 9.8 %copy-start.1 = (f32[32,3,544]{2,0,1:T(8,128)S(1)}, f32[32,3,544]{2,0,1:T(8,128)}, u32[]{:S(2)}) copy-start(f32[32,3,544]{2,0,1:T(8,128)} %param.10) | copy-start | bytes 626692
  4.8 10.7 %copy-start.2 = (f32[32,3,544]{2,0,1:T(8,128)S(1)}, f32[32,3,544]{2,0,1:T(8,128)}, u32[]{:S(2)}) copy-start(f32[32,3,544]{2,0,1:T(8,128)} %param.9) | copy-start | bytes 626692
  4.8 11.7 %copy-start.3 = (f32[64,3,256]{2,0,1:T(8,128)S(1)}, f32[64,3,256]{2,0,1:T(8,128)}, u32[]{:S(2)}) copy-start(f32[64,3,256]{2,0,1:T(8,128)} %param.16) | copy-start | bytes 589828
  4.8 11.7 %copy-start.5 = (f32[64,3,256]{2,0,1:T(8,128)S(1)}, f32[64,3,256]{2,0,1:T(8,128)}, u32[]{:S(2)}) copy-start(f32[64,3,256]{2,0,1:T(8,128)} %param.15) | copy-start | bytes 589828
  4.8 11.7 %copy-start.6 = (f32[64,256]{1,0:T(8,128)S(1)}, f32[64,256]{1,0:T(8,128)}, u32[]{:S(2)}) copy-start(f32[64,256]{1,0:T(8,128)} %param.17) | copy-start | bytes 196612
  4.8 90.7 %all-to-all-start = ((f32[1024,8,128]{2,1,0:T(8,128)}), f32[1024,8,128]{2,1,0:T(8,128)}, u32[]{:S(2)}, u32[]{:S(2)}) async-start(f32[1024,8,128]{2,1,0:T(8,128)} %bitcast.28), calls=%async_computation | async-start | bytes 8388608 | tf_op jit(solution)/shard_map/all_to_all | solution.py:444
  18.2 10.9 %copy-start.7 = (s32[32,8]{0,1:T(8,128)S(1)}, s32[32,8]{0,1:T(8,128)}, u32[]{:S(2)}) copy-start(s32[32,8]{0,1:T(8,128)} %param.14) | copy-start | bytes 3076
  18.2 11.6 %copy-start.8 = (s32[32,8]{0,1:T(8,128)S(1)}, s32[32,8]{0,1:T(8,128)}, u32[]{:S(2)}) copy-start(s32[32,8]{0,1:T(8,128)} %param.12) | copy-start | bytes 3076
  18.2 11.7 %copy-start.9 = (s32[32,8]{0,1:T(8,128)S(1)}, s32[32,8]{0,1:T(8,128)}, u32[]{:S(2)}) copy-start(s32[32,8]{0,1:T(8,128)} %param.13) | copy-start | bytes 3076
  28.3 0.8 copy-start
  166.5 9.3 %copy-start.4 = (f32[64,3,256]{2,0,1:T(8,128)S(1)}, f32[64,3,256]{2,0,1:T(8,128)}, u32[]{:S(2)}) copy-start(f32[64,3,256]{2,0,1:T(8,128)} %param.16) | copy-start | bytes 589828
